TPU v7x, 32 devices: a whole 2x2x4 slice. The times are simulated.
32 devices in a mesh: dp: 4 (over y, core), fsdp: 8 (over z, x).
Axes of the slice: x: 2, y: 2, z: 4, core: 2. Of those that a mesh axis runs over, the one named last changes fastest.
Arguments:
- tokens: bfloat16 [65536, 512], P(('dp', 'fsdp')), may hold values from -6 to 6
- grad_out: bfloat16 [65536, 512], P(('dp', 'fsdp')), may hold values from -6 to 6
- routes: int32 [65536, 8], P(('dp', 'fsdp')), may hold values from 0 to 23, all different within a row
- segments: int32 [64, 1024], P(('dp', 'fsdp')), may hold values from 0 to 3, never falling along the last dimension, each value on 1 to 512 neighbouring positions
- params: float32 [3748864], P(('dp', 'fsdp'))
- first_moment: float32 [3748864], P(('dp', 'fsdp'))
- second_moment: float32 [3748864], P(('dp', 'fsdp'))
- ema_weights: float32 [3748864], P(('dp', 'fsdp'))
Outputs:
- output: bfloat16 [65536, 512], P(('dp', 'fsdp'))
- input_grad: float32 [65536, 512], P(('dp', 'fsdp'))
- expert_load: float32 [24], replicated
- grad_norm: float32 [1], replicated
- new_params: float32 [3748864], P(('dp', 'fsdp'))
- new_first: float32 [3748864], P(('dp', 'fsdp'))
- new_second: float32 [3748864], P(('dp', 'fsdp'))
- new_ema: float32 [3748864], P(('dp', 'fsdp'))
- gain_grads: float32 [2, 512], replicated
Inputs may be any that keep to these rules, and one draw needn't show every extreme that they name: `routes`: each token names 8 different head experts. `segments`: document numbers never fall along a packed row.
All inputs are finite; a program needn't handle non-finite values.
Results may differ from a plain program's by a relative error of at most 0.012.
The roundings to bfloat16 on the way count: a program that leaves them out, or rounds other values in their place, can miss the bound.
Values may be sent and summed in bfloat16 or wider, within the bound.
A program may use at most 320 MiB of HBM per device.

v0:
```python
import copy
import functools
import itertools

import jax
import jax.numpy as jnp
from jax import lax
from jax.experimental import pallas as pl
from jax.experimental.pallas import tpu as pltpu
from jax.sharding import PartitionSpec as P

D = 512
E = 24
TOPK = 8
H = 64
FF = 2048
STEP = 10

NORM_EPS = 1e-06
CLIP_LIMIT = 1.0
BETA_FIRST = 0.9
BETA_SECOND = 0.95
LEARN_RATE = 0.1
DECAY_RATE = 0.1
ADAM_EPS = 1e-08
EMA_KEEP = 0.9
NEG_LARGE = -1e30

QW = E * H
KROW = QW
VROW = QW + H
RROW = QW + 2 * H
ALLW = 1696
LEN = 1024
TB = 512
NB = LEN // TB
QB = 128
SIDE = 4
MOST = 512 // QB + 1
SORT_STEPS = (
    (0, 1), (2, 3), (4, 5), (6, 7), (0, 2), (1, 3), (4, 6), (5, 7), (1, 2), (5, 6),
    (0, 4), (1, 5), (2, 6), (3, 7), (2, 4), (3, 5), (1, 2), (3, 4), (5, 6),
)
FC = 256
MB = 512
MIB = 1 << 20

WR_ROW = 8
WK_ROW = 104
WV_ROW = 360
WQ_ROW = 616
WO_ROW = 6760
W1_ROW = 12904
W2_ROW = 21096
ALL_ROWS = 29288
UNIT = 16 * 128
MESH = pl.DeviceIdType.MESH

F32 = jnp.float32
BF16 = jnp.bfloat16


def nn(a, b):
    return lax.dot_general(a, b, (((1,), (0,)), ((), ())), preferred_element_type=F32)


def nt(a, b):
    return lax.dot_general(a, b, (((1,), (1,)), ((), ())), preferred_element_type=F32)


def tn(a, b):
    return lax.dot_general(a, b, (((0,), (0,)), ((), ())), preferred_element_type=F32)


def rms_scale(values):
    return lax.rsqrt(jnp.mean(values * values, axis=-1, keepdims=True) + NORM_EPS)


def slot_of(routes, k, rows):
    return jnp.broadcast_to(routes[k : k + 1, :], (rows, routes.shape[1]))


def expert_rows(routes, k):
    return jnp.broadcast_to(routes.astype(jnp.int16)[k : k + 1, :], (16, routes.shape[1]))


def pick_heads(routes, source_ref, k):
    tokens = routes.shape[1]
    route = expert_rows(routes, k)
    taken = source_ref[k * H : (k + 1) * H, :].reshape(H // 16, 16, tokens)
    for e in range(k + 1, k + E - TOPK + 1):
        piece = source_ref[e * H : (e + 1) * H, :].reshape(H // 16, 16, tokens)
        taken = jnp.where((route == jnp.int16(e))[None], piece, taken)
    return taken.reshape(H, tokens)


def place_heads(routes, source_ref, target_ref):
    tokens = routes.shape[1]
    rows = [expert_rows(routes, k) for k in range(TOPK)]
    for e in range(E):
        total = jnp.zeros((H // 16, 16, tokens), BF16)
        for k in range(max(0, e - (E - TOPK)), min(TOPK - 1, e) + 1):
            piece = source_ref[k * H : (k + 1) * H, :].reshape(H // 16, 16, tokens)
            total = jnp.where((rows[k] == jnp.int16(e))[None], piece, total)
        target_ref[e * H : (e + 1) * H, :] = total.reshape(H, tokens)


def sorted_rows(rows):
    rows = list(rows)
    for one, two in SORT_STEPS:
        rows[one], rows[two] = jnp.minimum(rows[one], rows[two]), jnp.maximum(rows[one], rows[two])
    return rows


def key_mask(first_key, first_query, rows, start_row):
    keys = lax.broadcasted_iota(jnp.int32, (rows, QB), 0) + first_key
    queries = lax.broadcasted_iota(jnp.int32, (rows, QB), 1) + first_query
    mask = (keys <= queries) & (keys >= start_row)
    return jnp.concatenate([mask] * SIDE, axis=1)


def group_of(ref, k, lanes):
    return jnp.concatenate([ref[i * H : (i + 1) * H, lanes] for i in range(k, k + SIDE)], axis=1)


def row_group(ref, k, lanes):
    return jnp.concatenate([ref[i : i + 1, lanes] for i in range(k, k + SIDE)], axis=1)


def by_span(attend, row, place, segment_ref):
    def one(j, carry):
        block = place * (TB // QB) + j
        first = block * QB
        span = jnp.int32(1)
        for back in range(MOST - 1):
            last = first - back * QB - 1
            same = segment_ref[row, jnp.maximum(last, 0)] == segment_ref[row, first]
            span = span + jnp.where((last >= 0) & same, 1, 0)
        for blocks in range(1, MOST + 1):

            @pl.when(span == blocks)
            def _(blocks=blocks):
                attend(pl.ds(pl.multiple_of(j * QB, QB), QB), block, blocks)

        return carry

    lax.fori_loop(0, TB // QB, one, 0)


def head_forward_kernel(
    steps, segment_smem, x_ref, route_ref, segment_ref, wall_ref, gain_ref,
    q_ref, att_ref, gate_ref, lse_ref, kv_ref, kvt_ref, start_ref, sorted_ref, count_ref,
    all_scr, low_scr, k_scr, vt_scr, count_scr,
):
    step = pl.program_id(0)
    place = lax.rem(step, NB)
    here = pl.multiple_of(place * TB, TB)

    @pl.when(step == 0)
    def _():
        count_scr[...] = jnp.zeros_like(count_scr)

    row = segment_ref[pl.ds(lax.div(step, NB), 1), :]
    segments = segment_ref[pl.ds(lax.div(step, NB), 1), pl.ds(here, TB)]
    start = jnp.zeros((1, TB), jnp.int32)
    for number in range(1, 4):
        below = jnp.sum((row < number).astype(jnp.int32), axis=1, keepdims=True)
        start = jnp.where(segments == number, below, start)
    start_ref[...] = start
    x = x_ref[...].astype(F32)
    normed = (x * rms_scale(x) * gain_ref[...]).astype(BF16)
    all_scr[...] = nt(wall_ref[...], normed)
    kt = all_scr[KROW : KROW + H, :]
    vt = all_scr[VROW : VROW + H, :]
    logits = all_scr[RROW : RROW + E, :]
    kvt = jnp.concatenate([kt, vt], axis=0)
    kv = kvt.T.astype(BF16)
    kv_ref[...] = kv
    kvt_ref[...] = kvt.astype(BF16)
    k_scr[pl.ds(here, TB), :] = kv[:, :H]
    vt_scr[:, pl.ds(here, TB)] = vt.astype(BF16)
    routes = jnp.concatenate(sorted_rows(route_ref[k : k + 1, :] for k in range(TOPK)), axis=0)
    sorted_ref[...] = routes
    experts = lax.broadcasted_iota(jnp.int32, (E, TB), 0)
    chosen = []
    counts = count_scr[...]
    for k in range(TOPK):
        named = slot_of(routes, k, E) == experts
        chosen.append(jnp.sum(jnp.where(named, logits, 0.0), axis=0, keepdims=True))
        counts = counts + named.astype(F32)
    count_scr[...] = counts
    chosen = jnp.concatenate(chosen, axis=0)
    raised = jnp.exp(chosen - jnp.max(chosen, axis=0, keepdims=True))
    gate_ref[...] = raised / jnp.sum(raised, axis=0, keepdims=True)
    low_scr[...] = all_scr[0:QW, :].astype(BF16)
    for k in range(TOPK):
        q_ref[k * H : (k + 1) * H, :] = pick_heads(routes, low_scr, k) * jnp.asarray(H ** (-0.5), BF16)

    def attend(lanes, block, blocks):
        rows = blocks * QB
        first_key = pl.multiple_of((block - (blocks - 1)) * QB, QB)
        mask = key_mask(first_key, block * QB, rows, start_ref[:, lanes])
        keys = k_scr[pl.ds(first_key, rows), :]
        values = vt_scr[:, pl.ds(first_key, rows)]
        groups = [nn(keys, group_of(q_ref, 0, lanes))]
        for k in range(0, TOPK, SIDE):
            if k + SIDE < TOPK:
                groups.append(nn(keys, group_of(q_ref, k + SIDE, lanes)))
            scores = jnp.where(mask, groups[k // SIDE], NEG_LARGE)
            top = jnp.max(scores, axis=0, keepdims=True)
            raised = jnp.exp(scores - top)
            total = jnp.sum(raised, axis=0, keepdims=True)
            out = nn(values, (raised * (1.0 / total)).astype(BF16))
            lse = top + jnp.log(total)
            for side in range(SIDE):
                one = slice(side * QB, (side + 1) * QB)
                att_ref[(k + side) * H : (k + side + 1) * H, lanes] = out[:, one]
                lse_ref[k + side : k + side + 1, lanes] = lse[:, one]

    by_span(attend, lax.div(step, NB), place, segment_smem)

    @pl.when(step == steps - 1)
    def _():
        held = jnp.sum(count_scr[...], axis=1, keepdims=True)
        lane = lax.broadcasted_iota(jnp.int32, (E, 128), 1)
        row = lax.broadcasted_iota(jnp.int32, (E, 128), 0)
        count_ref[...] = jnp.sum(jnp.where(lane == row, held, 0.0), axis=0, keepdims=True)


def picks(rows, stride, first):
    at = lax.broadcasted_iota(jnp.int32, (rows, D), 1)
    row = lax.broadcasted_iota(jnp.int32, (rows, D), 0)
    return (at == row * stride + first).astype(F32)


def exact(product, a, b):
    return lax.dot_general(
        a, b, (product, ((), ())), precision=lax.Precision.HIGHEST, preferred_element_type=F32
    )


def gelu_parts(v):
    cdf = 0.5 + 0.5 * lax.erf(v * 0.7071067811865476)
    return cdf, jnp.exp(v * v * -0.5) * 0.3989422804014327


def middle_kernel(
    x_ref, dy_ref, gain_ref, wo_ref, w1_ref, w2_ref, route_ref, gate_ref, att_ref,
    out_ref, dres_ref, datt_ref, delta_ref, dlogit_ref, flat_ref, extra_ref, dgain_ref,
    slot_scr, head_scr, mix_scr, hidden_scr, dpre_scr, w1t_scr, w2t_scr, dwo_ref, dw1_ref, dw2t_ref, rows_scr, low_scr, row_sem,
):
    step = pl.program_id(0)

    @pl.when(step == 0)
    def _():
        dwo_ref[...] = jnp.zeros_like(dwo_ref)
        dw1_ref[...] = jnp.zeros_like(dw1_ref)
        dw2t_ref[...] = jnp.zeros_like(dw2t_ref)
        for first in range(0, FF, 512):
            part = slice(first, first + 512)
            w1t_scr[part, :] = w1_ref[:, part].T
            w2t_scr[:, part] = w2_ref[part, :].T
        dgain_ref[...] = jnp.zeros_like(dgain_ref)

    routes = route_ref[...]
    tokens = routes.shape[1]
    gates = gate_ref[...]
    for k in range(TOPK):
        rows = slice(k * H, (k + 1) * H)
        slot_scr[rows, :] = (gates[k : k + 1, :] * att_ref[rows, :]).astype(BF16)
    place_heads(routes, slot_scr, mix_scr)
    x = x_ref[...].astype(F32)
    dy = dy_ref[...]
    mixed = mix_scr[...]
    residual = x + tn(mixed, wo_ref[...])
    scale = rms_scale(residual)
    gain = gain_ref[...]
    second = (residual * scale * gain).astype(BF16)
    second_t = second.T
    dy_t = dy.T
    pre = [nn(second, w1_ref[:, 0:FC])]
    back = [nn(dy, w2t_scr[:, 0:FC])]
    for i in range(FF // FC):
        here = slice(i * FC, (i + 1) * FC)
        if i + 1 < FF // FC:
            after = slice((i + 1) * FC, (i + 2) * FC)
            pre.append(nn(second, w1_ref[:, after]))
            back.append(nn(dy, w2t_scr[:, after]))
        cdf, density = gelu_parts(pre[i])
        hidden_scr[:, here] = (pre[i] * cdf).astype(BF16)
        dpre_scr[:, here] = (back[i] * (cdf + pre[i] * density)).astype(BF16)
    dsecond = nn(dpre_scr[...], w1t_scr[...])
    out_ref[...] = (residual + nn(hidden_scr[...], w2_ref[...])).astype(BF16)
    dw1_ref[...] += nn(second_t, dpre_scr[...])
    dw2t_ref[...] += nn(dy_t, hidden_scr[...])
    dgain_ref[...] += jnp.sum(dsecond * residual * scale, axis=0, keepdims=True)
    weighted = gain * dsecond
    dres = (
        dy.astype(F32)
        + scale * weighted
        - residual * (scale * scale * scale) * jnp.mean(weighted * residual, axis=-1, keepdims=True)
    )
    dres_ref[...] = dres
    branch = dres.astype(BF16)
    dwo_ref[...] += nn(mixed, branch)
    head_scr[...] = nt(wo_ref[...], branch).astype(BF16)
    dgates = []
    for k in range(TOPK):
        rows = slice(k * H, (k + 1) * H)
        dslot = pick_heads(routes, head_scr, k).astype(F32)
        attended = att_ref[rows, :]
        dgates.append(jnp.sum(dslot * attended, axis=0, keepdims=True))
        datt = (gates[k : k + 1, :] * dslot).astype(BF16)
        datt_ref[rows, :] = datt
        delta_ref[k : k + 1, :] = jnp.sum(datt.astype(F32) * attended, axis=0, keepdims=True)
    dgate = jnp.concatenate(dgates, axis=0)
    dchosen = gates * (dgate - jnp.sum(gates * dgate, axis=0, keepdims=True))
    experts = lax.broadcasted_iota(jnp.int32, (E, tokens), 0)
    dlogits = jnp.zeros((E, tokens), F32)
    for k in range(TOPK):
        dlogits = jnp.where(
            slot_of(routes, k, E) == experts,
            jnp.broadcast_to(dchosen[k : k + 1, :], (E, tokens)),
            dlogits,
        )
    dlogit_ref[...] = dlogits

    @pl.when(step == pl.num_programs(0) - 1)
    def _():
        last = low_scr.shape[0]
        ends = (0, (W1_ROW - WO_ROW - 8) // 16 * 16, (W2_ROW - WO_ROW - 8) // 16 * 16, last)

        def out(number):
            first, count = ends[number], ends[number + 1] - ends[number]
            return pltpu.make_async_copy(
                low_scr.at[pl.ds(first, count), :],
                flat_ref.at[pl.ds(WO_ROW + 8 + first, count), :],
                row_sem.at[number],
            )

        def leave(number):
            first, count = ends[number], ends[number + 1] - ends[number]
            low_scr[pl.ds(first, count), :] = rows_scr[pl.ds(first + 8, count), :].astype(BF16)
            out(number).start()

        for c in range(D // 128):
            rows_scr[pl.ds(c, QW, stride=4), :] = dwo_ref[:, c * 128 : (c + 1) * 128]
        extra_ref[...] = rows_scr[0:8, :]
        leave(0)
        for c in range(FF // 128):
            rows_scr[pl.ds(W1_ROW - WO_ROW + c, D, stride=16), :] = dw1_ref[:, c * 128 : (c + 1) * 128]
        leave(1)
        for c in range(D // 128):
            rows_scr[pl.ds(W2_ROW - WO_ROW + c, FF, stride=4), :] = dw2t_ref[c * 128 : (c + 1) * 128, :].T
        leave(2)
        for number in range(3):
            out(number).wait()


def head_backward_kernel(
    segment_smem, x_ref, gain_ref, wall_ref, route_ref, start_ref, q_ref, datt_ref,
    lse_ref, delta_ref, kv_ref, kvt_ref, dlogit_ref, dres_ref, dgain_two_ref, extra_ref, flat_in,
    dx_ref, flat_ref,
    dk_scr, dv_scr, dq_scr, dall_scr, prob_scr, dscore_scr, dwall_ref, dgain_ref, rows_scr, low_scr, row_sem,
):
    step = pl.program_id(0)
    place = NB - 1 - lax.rem(step, NB)
    here = pl.multiple_of(place * TB, TB)

    @pl.when(step == 0)
    def _():
        dwall_ref[...] = jnp.zeros_like(dwall_ref)
        dgain_ref[...] = jnp.zeros_like(dgain_ref)

    @pl.when(lax.rem(step, NB) == 0)
    def _():
        dk_scr[...] = jnp.zeros_like(dk_scr)
        dv_scr[...] = jnp.zeros_like(dv_scr)

    def attend(lanes, block, blocks):
        rows = blocks * QB
        first_key = pl.multiple_of((block - (blocks - 1)) * QB, QB)
        mask = key_mask(first_key, block * QB, rows, start_ref[:, lanes])
        keys = kv_ref[pl.ds(first_key, rows), :H]
        values = kv_ref[pl.ds(first_key, rows), H:]
        keys_t = kvt_ref[:H, pl.ds(first_key, rows)]
        queries = [group_of(q_ref, k, lanes) for k in range(0, TOPK, SIDE)]
        datts = [group_of(datt_ref, k, lanes) for k in range(0, TOPK, SIDE)]
        scores = [nn(keys, queries[0])]
        dprobs = [nn(values, datts[0])]
        for i in range(TOPK // SIDE):
            if i + 1 < TOPK // SIDE:
                scores.append(nn(keys, queries[i + 1]))
                dprobs.append(nn(values, datts[i + 1]))
            k = i * SIDE
            wide = slice(k * QB, (k + SIDE) * QB)
            probs = jnp.exp(jnp.where(mask, scores[i], NEG_LARGE) - row_group(lse_ref, k, lanes))
            dscore = (probs * (dprobs[i] - row_group(delta_ref, k, lanes))).astype(BF16)
            prob_scr[0:rows, wide] = probs.astype(BF16)
            dscore_scr[0:rows, wide] = dscore
            dq = (nn(keys_t, dscore) * (H ** (-0.5))).astype(BF16)
            for side in range(SIDE):
                dq_scr[(k + side) * H : (k + side + 1) * H, lanes] = dq[:, side * QB : (side + 1) * QB]
        dv_scr[pl.ds(first_key, rows), :] += nt(prob_scr[0:rows, :], jnp.concatenate(datts, axis=1))
        dk_scr[pl.ds(first_key, rows), :] += nt(dscore_scr[0:rows, :], jnp.concatenate(queries, axis=1))

    by_span(attend, lax.div(step, NB), place, segment_smem)
    place_heads(route_ref[...], dq_scr, dall_scr)
    dkv = jnp.concatenate([dk_scr[pl.ds(here, TB), :], dv_scr[pl.ds(here, TB), :]], axis=1)
    dall_scr[KROW : KROW + 2 * H, :] = dkv.T.astype(BF16)
    dall_scr[RROW : RROW + 32, :] = jnp.concatenate(
        [dlogit_ref[...], jnp.zeros((32 - E, TB), F32)], axis=0
    ).astype(BF16)
    x = x_ref[...].astype(F32)
    scale = rms_scale(x)
    gain = gain_ref[...]
    normed = (x * scale * gain).astype(BF16)
    dall = dall_scr[...]
    dwall_ref[...] += nn(dall, normed)
    dnormed = tn(dall, wall_ref[...])
    dgain_ref[...] += jnp.sum(dnormed * x * scale, axis=0, keepdims=True)
    weighted = gain * dnormed
    dx_ref[...] = (
        dres_ref[...]
        + scale * weighted
        - x * (scale * scale * scale) * jnp.mean(weighted * x, axis=-1, keepdims=True)
    )

    @pl.when(step == pl.num_programs(0) - 1)
    def _():
        for c in range(D // 128):
            lanes = slice(c * 128, (c + 1) * 128)
            rows_scr[c : c + 1, :] = dgain_ref[:, lanes]
            rows_scr[4 + c : 5 + c, :] = dgain_two_ref[:, lanes]
        router_t = dwall_ref[RROW : RROW + E, :]
        across = jnp.concatenate(
            [exact(((1,), (1,)), router_t, picks(32, 16, b)) for b in range(16)], axis=0
        ).T
        for j in range(3):
            rows_scr[pl.ds(WR_ROW + j, 32, stride=3), :] = across[:, j * 128 : (j + 1) * 128]
        for first, row in ((KROW, WK_ROW), (VROW, WV_ROW)):
            part = dwall_ref[first : first + H, :]
            rows_scr[row : row + 256, :] = jnp.concatenate(
                [exact(((1,), (1,)), picks(256, 2, b), part) for b in range(2)], axis=1
            )
        for c in range(QW // 128):
            rows_scr[pl.ds(WQ_ROW + c, D, stride=12), :] = dwall_ref[c * 128 : (c + 1) * 128, :].T
        rows_scr[WO_ROW : WO_ROW + 8, :] = extra_ref[...]
        low_scr[...] = rows_scr[...].astype(BF16)
        copy = pltpu.make_async_copy(low_scr, flat_ref.at[pl.ds(0, WO_ROW + 8), :], row_sem.at[0])
        copy.start()
        copy.wait()


def whole(shape):
    return pl.BlockSpec(shape, lambda *_: (0,) * len(shape), pipeline_mode=pl.Buffered(1))


def kept(shape):
    return pl.BlockSpec(shape, lambda *_: (0,) * len(shape))


SMEM = pl.BlockSpec(memory_space=pltpu.SMEM)


def struct(shape, kind=F32):
    return jax.ShapeDtypeStruct(shape, kind)


def params_for(mib):
    return pltpu.CompilerParams(vmem_limit_bytes=mib * MIB)


def head_forward(tokens, routes_t, segments, wall, gain):
    count = tokens.shape[0]
    steps = count // TB
    across = lambda rows: pl.BlockSpec((rows, TB), lambda b: (0, b))
    down = lambda columns: pl.BlockSpec((TB, columns), lambda b: (b, 0))
    return pl.pallas_call(
        functools.partial(head_forward_kernel, steps),
        grid=(steps,),
        in_specs=[SMEM, down(D), across(TOPK), whole(segments.shape), whole((ALLW, D)), whole((1, D))],
        out_specs=[
            across(TOPK * H), across(TOPK * H), across(TOPK), across(TOPK), down(2 * H), across(2 * H),
            across(1), across(TOPK), whole((1, 128)),
        ],
        scratch_shapes=[
            pltpu.VMEM((ALLW, TB), F32),
            pltpu.VMEM((QW, TB), BF16),
            pltpu.VMEM((LEN, H), BF16),
            pltpu.VMEM((H, LEN), BF16),
            pltpu.VMEM((E, TB), F32),
        ],
        out_shape=[
            struct((TOPK * H, count), BF16),
            struct((TOPK * H, count)),
            struct((TOPK, count)),
            struct((TOPK, count)),
            struct((count, 2 * H), BF16),
            struct((2 * H, count), BF16),
            struct((1, count), jnp.int32),
            struct((TOPK, count), jnp.int32),
            struct((1, 128)),
        ],
        compiler_params=params_for(56),
        name="head_forward",
        cost_estimate=pl.CostEstimate(flops=10_000_000_000, bytes_accessed=16_000_000, transcendentals=0),
    )(segments, tokens, routes_t, segments, wall, gain)


def middle(flat_rows, tokens, grad_out, gain, wo, w1, w2, routes_t, gates, attended):
    count = tokens.shape[0]
    steps = count // MB
    across = lambda rows: pl.BlockSpec((rows, MB), lambda b: (0, b))
    down = lambda columns: pl.BlockSpec((MB, columns), lambda b: (b, 0))
    return pl.pallas_call(
        middle_kernel,
        grid=(steps,),
        in_specs=[
            down(D), down(D), whole((1, D)), whole((QW, D)), whole((D, FF)), whole((FF, D)),
            across(TOPK), across(TOPK), across(TOPK * H),
        ],
        out_specs=[
            down(D), down(D), across(TOPK * H), across(TOPK), across(E),
            pl.BlockSpec(memory_space=pl.ANY), whole((8, 128)), whole((1, D)),
        ],
        out_shape=[
            struct((count, D), BF16),
            struct((count, D)),
            struct((TOPK * H, count), BF16),
            struct((TOPK, count)),
            struct((E, count)),
            struct((flat_rows, 128), BF16),
            struct((8, 128)),
            struct((1, D)),
        ],
        scratch_shapes=[
            pltpu.VMEM((TOPK * H, MB), BF16),
            pltpu.VMEM((QW, MB), BF16),
            pltpu.VMEM((QW, MB), BF16),
            pltpu.VMEM((MB, FF), BF16),
            pltpu.VMEM((MB, FF), BF16),
            pltpu.VMEM((FF, D), BF16),
            pltpu.VMEM((D, FF), BF16),
            pltpu.VMEM((QW, D), F32),
            pltpu.VMEM((D, FF), F32),
            pltpu.VMEM((D, FF), F32),
            pltpu.VMEM((flat_rows - WO_ROW, 128), F32),
            pltpu.VMEM((flat_rows - WO_ROW - 8, 128), BF16),
            pltpu.SemaphoreType.DMA((3,)),
        ],
        compiler_params=params_for(60),
        name="middle",
    )(tokens, grad_out, gain, wo, w1, w2, routes_t, gates, attended)


def head_backward(
    segments, tokens, gain, wall, routes_t, start, queries, datt, lse, delta, kv, kvt, dlogits, dres,
    dgain_two, extra, flat,
):
    count = tokens.shape[0]
    steps = count // TB

    def place(b):
        return (b // NB) * NB + NB - 1 - b % NB

    across = lambda rows: pl.BlockSpec((rows, TB), lambda b: (0, place(b)))
    down = lambda columns: pl.BlockSpec((TB, columns), lambda b: (place(b), 0))
    return pl.pallas_call(
        head_backward_kernel,
        grid=(steps,),
        in_specs=[
            SMEM, down(D), whole((1, D)), whole((ALLW, D)), across(TOPK), across(1),
            across(TOPK * H), across(TOPK * H), across(TOPK), across(TOPK),
            pl.BlockSpec((LEN, 2 * H), lambda b: (b // NB, 0)),
            pl.BlockSpec((2 * H, LEN), lambda b: (0, b // NB)),
            across(E), down(D), whole((1, D)), whole((8, 128)), pl.BlockSpec(memory_space=pl.ANY),
        ],
        out_specs=[down(D), pl.BlockSpec(memory_space=pl.ANY)],
        scratch_shapes=[
            pltpu.VMEM((LEN, H), F32),
            pltpu.VMEM((LEN, H), F32),
            pltpu.VMEM((TOPK * H, TB), BF16),
            pltpu.VMEM((ALLW, TB), BF16),
            pltpu.VMEM((MOST * QB, TOPK * QB), BF16),
            pltpu.VMEM((MOST * QB, TOPK * QB), BF16),
            pltpu.VMEM((ALLW, D), F32),
            pltpu.VMEM((1, D), F32),
            pltpu.VMEM((WO_ROW + 8, 128), F32),
            pltpu.VMEM((WO_ROW + 8, 128), BF16),
            pltpu.SemaphoreType.DMA((1,)),
        ],
        out_shape=[struct((count, D)), struct(flat.shape, BF16)],
        input_output_aliases={16: 1},
        compiler_params=params_for(56),
        name="head_backward",
        cost_estimate=pl.CostEstimate(flops=30_000_000_000, bytes_accessed=24_000_000, transcendentals=0),
    )(
        segments, tokens, gain, wall, routes_t, start, queries, datt, lse, delta, kv, kvt, dlogits, dres,
        dgain_two, extra, flat,
    )


class Mesh3:
    def __init__(self, shards, over):
        shard = lax.axis_index("dp")
        other = lax.axis_index("fsdp")
        self.over = over
        self.many = shards * over
        self.sizes = {"x": 2, "y": shards // 2, "z": over // 2}
        self.here = {"x": lax.rem(other, 2), "y": lax.div(shard, 2), "z": lax.div(other, 2)}
        self.core = lax.rem(shard, 2)
        self.me = shard * over + other
        self.partner = (shard + 1 - 2 * self.core, other)

    def at_z(self, z):
        same = copy.copy(self)
        if z is not None:
            same.here = dict(self.here, z=z)
        return same

    def spots(self):
        x, y, z = (self.sizes[axis] for axis in "xyz")
        return list(itertools.product(range(x), range(y), range(1 - z, z)))

    def round_spots(self):
        return list(itertools.product(*[range(self.sizes[axis]) for axis in "xyz"]))

    def exists(self, z_steps):
        place = self.here["z"] + z_steps
        if isinstance(place, int):
            return 0 <= place < self.sizes["z"]
        return (place >= 0) & (place < self.sizes["z"])

    def device(self, core, spot):
        size = self.sizes["z"]
        x = lax.rem(self.here["x"] + spot[0], self.sizes["x"])
        y = lax.rem(self.here["y"] + spot[1], self.sizes["y"])
        z = self.here["z"] + spot[2]
        z = z % size if isinstance(z, int) else lax.rem(z + size, size)
        return (y * 2 + core, z * 2 + x)

    def number(self, core, spot):
        shard, other = self.device(core, spot)
        return shard * self.over + other

    def greet(self, devices):
        barrier = pltpu.get_barrier_semaphore()
        for device in devices:
            pl.semaphore_signal(barrier, inc=1, device_id=device, device_id_type=MESH)
        pl.semaphore_wait(barrier, len(devices))

    def near(self):
        steps = [at(axis, step) for axis in "xyz" for step in range(1, self.sizes[axis])]
        return [self.device(self.core, step) for step in steps] + [self.partner]

    def column(self):
        steps = [(core, step) for core in range(2) for step in range(self.sizes["z"]) if core or step]
        return [self.device(lax.rem(self.core + core, 2), (0, 0, step)) for core, step in steps]

    def layer(self):
        steps = [(x, y, 0) for x in range(self.sizes["x"]) for y in range(self.sizes["y"]) if x or y]
        return [self.device(self.core, step) for step in steps]


def at(axis, step):
    return tuple(step if one == axis else 0 for one in "xyz")


def last_axis(axes, spot):
    return max([i for i, axis in enumerate(axes) if spot["xyz".index(axis)]], default=-1)


def pieces_of(window, count=2):
    if window < 512:
        return [(0, window)]
    ends = [window // 16 * i // count * 16 for i in range(count)] + [window]
    return [(first, last - first) for first, last in zip(ends, ends[1:])]


def act(condition, action):
    if condition is True:
        action()
    elif condition is not False:
        pl.when(condition)(action)


GATHER_AXES = (("zxy", "yzx"), ("zyx", "xzy"))
REDUCE_PIECES = 3
REDUCE_AXES = ("zxy", "zyx")


def onward(mesh, axes, spot):
    last = last_axis(axes, spot)
    steps = []
    if last >= 0 and axes[last] == "z":
        steps.append(("z", -1 if spot[2] > 0 else 1))
    for axis in axes[last + 1 :]:
        steps += [("z", 1), ("z", -1)] if axis == "z" else [
            (axis, one) for one in range(1, mesh.sizes[axis])
        ]
    return steps


def gather_own_core(mesh, core, land, send_sem, recv_sem, begin):
    window = land.shape[1]
    pieces = pieces_of(window)
    slots = {}
    events = []

    def moved(owner, device, slot, p):
        rows = pl.ds(*pieces[p])
        return pltpu.make_async_remote_copy(
            src_ref=land.at[owner, rows],
            dst_ref=land.at[owner, rows],
            send_sem=send_sem.at[slot, p],
            recv_sem=recv_sem.at[owner, p],
            device_id=device,
            device_id_type=MESH,
        )

    for spot in mesh.spots():
        there = mesh.exists(spot[2])
        if there is False:
            continue
        owner = mesh.number(core, spot)
        turn = 0.5 * abs(spot[2]) + (spot[0] > 0) + (spot[1] > 0) + (0.001 if spot[2] < 0 else 0)
        for p in range(len(pieces)):
            sends = []
            for axis, step in onward(mesh, GATHER_AXES[core][p], spot):
                key = (spot[0], spot[1], spot[2] % mesh.sizes["z"], axis, step)
                away = mesh.exists(step) if axis == "z" else True
                if away is not False:
                    slot = slots.setdefault(key, len(slots))
                    sends.append((mesh.device(core, at(axis, step)), slot, away))
            key = (spot[0], spot[1], spot[2] % mesh.sizes["z"])
            sends.append((mesh.partner, slots.setdefault(key, len(slots)), True))

            def come(owner=owner, spot=spot, p=p, sends=sends):
                if any(spot):
                    moved(owner, mesh.partner, 0, p).wait_recv()
                for device, slot, away in sends:
                    act(away, moved(owner, device, slot, p).start)

            def done(owner=owner, p=p, sends=sends):
                for _, slot, away in sends:
                    act(away, moved(owner, mesh.partner, slot, p).wait_send)

            events.append((turn + 0.01 * p, there, come if begin else done))
    for _, there, action in sorted(events, key=lambda one: one[0]):
        act(there, action)


def gather_blocks(mesh, land, send_sem, recv_sem, begin):
    known = range(mesh.sizes["z"]) if mesh.sizes["z"] <= 4 else [None]
    for core in range(2):
        for z in known:

            @pl.when((mesh.core == core) & (True if z is None else mesh.here["z"] == z))
            def _(core=core, z=z):
                gather_own_core(mesh.at_z(z), core, land, send_sem, recv_sem, begin)


def each_owner(mesh, core, action):
    def one(number, carry):
        shard = 2 * lax.div(number, mesh.over) + core
        action(shard * mesh.over + lax.rem(number, mesh.over))
        return carry

    lax.fori_loop(0, mesh.many // 2, one, 0)


def reduce_blocks(mesh, core, source, mine, outgo, income, send_sem, recv_sem, total_ref):
    pieces = pieces_of(outgo.shape[1], REDUCE_PIECES)
    half = mesh.many // 2
    held = {spot: i for i, spot in enumerate(mesh.round_spots())}

    def across(kind, spot):
        slot = held[spot]
        return pltpu.make_async_remote_copy(
            src_ref=source(mesh.number(kind, spot)),
            dst_ref=income.at[slot],
            send_sem=send_sem.at[slot, 0],
            recv_sem=recv_sem.at[slot, 0],
            device_id=mesh.partner,
            device_id_type=MESH,
        )

    def moved(spot, p, device):
        rows = pl.ds(*pieces[p])
        slot = half + held[spot]
        return pltpu.make_async_remote_copy(
            src_ref=outgo.at[held[spot], rows],
            dst_ref=income.at[slot, rows],
            send_sem=send_sem.at[slot, p],
            recv_sem=recv_sem.at[slot, p],
            device_id=device,
            device_id_type=MESH,
        )

    def far(spot):
        z = {0: 0, 1: 3, 2: 5, 3: 8}.get(spot[2], 2 * spot[2] + 2)
        return z + 2 * (spot[0] > 0) + 2 * (spot[1] > 0)

    for spot in sorted(held, key=far, reverse=True):
        across(1 - core, spot).start()
    axes = REDUCE_AXES[core]
    order = sorted(
        itertools.product(held, range(len(pieces))), key=lambda one: 2 * one[1] / len(pieces) - 2 * far(one[0])
    )
    for spot, p in order:
        if p == 0:
            across(core, spot).wait_recv()
        rows = pl.ds(*pieces[p])
        total = mine(mesh.number(core, spot), *pieces[p]) + income[held[spot], rows].astype(F32)
        last = last_axis(axes, spot)
        for axis in axes[last + 1 :]:
            size = mesh.sizes[axis]
            for step in range(1, size):
                child = tuple(one or other for one, other in zip(spot, at(axis, size - step)))
                moved(child, p, mesh.partner).wait_recv()
                total = total + income[half + held[child], rows].astype(F32)
        if last < 0:
            total_ref[rows, :] = total
        else:
            outgo[held[spot], rows] = total.astype(BF16)
            step = spot["xyz".index(axes[last])]
            moved(spot, p, mesh.device(core, at(axes[last], step))).start()
    for spot, p in order:
        if p == 0:
            across(1 - core, spot).wait_send()
        if any(spot):
            moved(spot, p, mesh.partner).wait_send()


def sum_all(mesh, mine, stats, send_sem, recv_sem):
    column = mesh.sizes["z"] * 2
    layer = mesh.sizes["x"] * mesh.sizes["y"]
    groups = (
        (0, column, mesh.here["z"] * 2 + mesh.core, mesh.column()),
        (column, layer, mesh.here["x"] * mesh.sizes["y"] + mesh.here["y"], mesh.layer()),
    )
    total = mine
    for base, size, here, devices in groups:
        stats[base + here] = total

        def sent(j, device, base=base, here=here):
            return pltpu.make_async_remote_copy(
                src_ref=stats.at[base + here],
                dst_ref=stats.at[base + here],
                send_sem=send_sem.at[base + j],
                recv_sem=recv_sem.at[base + here],
                device_id=device,
                device_id_type=MESH,
            )

        def come(place, base=base):
            return pltpu.make_async_remote_copy(
                src_ref=stats.at[base + place],
                dst_ref=stats.at[base + place],
                send_sem=send_sem.at[base],
                recv_sem=recv_sem.at[base + place],
                device_id=mesh.partner,
                device_id_type=MESH,
            )

        for j, device in enumerate(devices):
            sent(j, device).start()
        for j in range(1, size):
            come(lax.rem(here + j, size)).wait_recv()
        for j, device in enumerate(devices):
            sent(j, device).wait_send()
        total = stats[base]
        for place in range(1, size):
            total = total + stats[base + place]
    return total


def window_rows(shard_size, many):
    units = [(shard_size * d) // UNIT for d in range(many + 1)]
    return 16 * (max(b - a for a, b in zip(units, units[1:])) + 1)


def first_row(shard_size, number):
    if isinstance(number, int):
        return number * shard_size // UNIT * 16
    return pl.multiple_of(lax.div(number * shard_size, UNIT) * 16, 16)


def inner_units(shard_size, many):
    units = [(shard_size * d) // UNIT for d in range(many + 1)]
    return min(b - a for a, b in zip(units, units[1:]))


def lay_inner(shard_size, many, land, flat, owner):
    count = 16 * inner_units(shard_size, many) - 16
    row = pl.multiple_of(first_row(shard_size, owner) + 16, 16)
    flat[pl.ds(row, count), :] = land[owner, pl.ds(16, count), :].astype(F32)


def lay_edges(shard_size, many, land, flat):
    inner = 16 * inner_units(shard_size, many)
    flat[0:16, :] = jnp.zeros((16, 128), F32)

    def lay(number, carry):
        row = first_row(shard_size, number)
        after = first_row(shard_size, number + 1)
        flat[pl.ds(row, 16), :] += land[number, 0:16, :].astype(F32)
        tail = land[number, pl.ds(inner, 16), :].astype(F32)
        flat[pl.ds(pl.multiple_of(row + inner, 16), 16), :] = tail
        last = pl.multiple_of(after - row, 16)
        flat[pl.ds(after, 16), :] = land[number, pl.ds(last, 16), :].astype(F32)
        return carry

    lax.fori_loop(0, many, lay, 0)


def early_matrices(flat, wall_ref, gain_one_ref, gain_two_ref):
    for c in range(D // 128):
        lanes = slice(c * 128, (c + 1) * 128)
        gain_one_ref[:, lanes] = flat[c : c + 1, :]
        gain_two_ref[:, lanes] = flat[4 + c : 5 + c, :]
    for c in range(QW // 128):
        wall_ref[c * 128 : (c + 1) * 128, :] = flat[pl.ds(WQ_ROW + c, D, stride=12), :].T.astype(BF16)
    for first, row in ((KROW, WK_ROW), (VROW, WV_ROW)):
        pair = flat[row : row + 256, :].T.astype(BF16)
        wall_ref[first : first + H, :] = (
            nn(pair[:H], picks(256, 2, 0).astype(BF16)) + nn(pair[H:], picks(256, 2, 1).astype(BF16))
        ).astype(BF16)
    across = jnp.concatenate(
        [flat[pl.ds(WR_ROW + j, 32, stride=3), :] for j in range(3)], axis=1
    ).T.astype(BF16)
    router_t = jnp.zeros((E, D), F32)
    for part in range(16):
        router_t = router_t + nn(across[part * E : (part + 1) * E, :], picks(32, 16, part).astype(BF16))
    wall_ref[RROW:ALLW, :] = jnp.concatenate(
        [router_t, jnp.zeros((ALLW - RROW - E, D), F32)], axis=0
    ).astype(BF16)


def gather_kernel(
    mesh, shard_size, own_ref,
    wall_out, gain_one_ref, gain_two_ref, wo_out, w1_out, w2_out,
    land, flat, wall_ref, wo_ref, w1_ref, w2_ref, send_sem, recv_sem, out_sem,
):
    mesh = mesh()
    many = mesh.many
    mesh.greet(mesh.near())
    land[mesh.me] = own_ref[...].astype(BF16)
    gather_blocks(mesh, land, send_sem, recv_sem, True)
    each_owner(mesh, mesh.core, functools.partial(lay_inner, shard_size, many, land, flat))

    def arrive(owner):
        for p in range(recv_sem.shape[1]):
            rows = pl.ds(*pieces_of(own_ref.shape[0])[p])
            pltpu.make_async_remote_copy(
                src_ref=land.at[owner, rows],
                dst_ref=land.at[owner, rows],
                send_sem=send_sem.at[0, p],
                recv_sem=recv_sem.at[owner, p],
                device_id=mesh.partner,
                device_id_type=MESH,
            ).wait_recv()
        lay_inner(shard_size, many, land, flat, owner)

    each_owner(mesh, 1 - mesh.core, arrive)
    lay_edges(shard_size, many, land, flat)
    copies = []

    def leave(matrix, out):
        one = pltpu.make_async_copy(matrix, out, out_sem.at[len(copies)])
        one.start()
        copies.append(one)

    for c in range(D // 128):
        wo_ref[:, c * 128 : (c + 1) * 128] = flat[pl.ds(WO_ROW + c, QW, stride=4), :].astype(BF16)
    leave(wo_ref, wo_out)
    for c in range(D // 128):
        w2_ref[:, c * 128 : (c + 1) * 128] = flat[pl.ds(W2_ROW + c, FF, stride=4), :].astype(BF16)
    leave(w2_ref, w2_out)
    for c in range(FF // 128):
        w1_ref[:, c * 128 : (c + 1) * 128] = flat[pl.ds(W1_ROW + c, D, stride=16), :].astype(BF16)
    leave(w1_ref, w1_out)
    early_matrices(flat, wall_ref, gain_one_ref, gain_two_ref)
    leave(wall_ref, wall_out)
    gather_blocks(mesh, land, send_sem, recv_sem, False)
    for one in copies:
        one.wait()


def gather_weights(shards, over, shard_size, own):
    window = own.shape[0]
    many = shards * over
    rows = (shard_size * (many - 1)) // UNIT * 16 + window
    vmem = pl.BlockSpec(memory_space=pltpu.VMEM)
    hbm = pl.BlockSpec(memory_space=pl.ANY)
    mesh = functools.partial(Mesh3, shards, over)
    pieces = len(pieces_of(window))
    return pl.pallas_call(
        functools.partial(gather_kernel, mesh, shard_size),
        in_specs=[vmem],
        out_specs=[hbm, vmem, vmem, hbm, hbm, hbm],
        out_shape=[
            struct((ALLW, D), BF16),
            struct((1, D)),
            struct((1, D)),
            struct((QW, D), BF16),
            struct((D, FF), BF16),
            struct((FF, D), BF16),
        ],
        scratch_shapes=[
            pltpu.VMEM((many, window, 128), BF16),
            pltpu.VMEM((rows, 128), F32),
            pltpu.VMEM((ALLW, D), BF16),
            pltpu.VMEM((QW, D), BF16),
            pltpu.VMEM((D, FF), BF16),
            pltpu.VMEM((FF, D), BF16),
            pltpu.SemaphoreType.DMA((5 * many // 2, pieces)),
            pltpu.SemaphoreType.DMA((many, pieces)),
            pltpu.SemaphoreType.DMA((4,)),
        ],
        compiler_params=pltpu.CompilerParams(
            collective_id=0, has_side_effects=True, vmem_limit_bytes=60 * MIB
        ),
        name="gather_weights",
    )(own)


def reduce_kernel(
    mesh, shard_size, flat_ref, count_ref,
    out_ref, total_ref, gain_ref,
    part, outgo, income, whole_scr, stats, part_sem, send_sem, recv_sem, stat_send, stat_recv,
):
    mesh = mesh()
    window = outgo.shape[1]
    span = part.shape[1]

    def source(owner):
        return flat_ref.at[pl.ds(first_row(shard_size, owner), window), :]

    def fetch(y):
        first = first_row(shard_size, (2 * y + mesh.core) * mesh.over)
        return pltpu.make_async_copy(flat_ref.at[pl.ds(first, span), :], part.at[y], part_sem.at[y])

    def mine(owner, first, rows):
        shard = lax.div(owner, mesh.over)
        row = first_row(shard_size, owner) - first_row(shard_size, shard * mesh.over) + first
        return part[lax.div(shard, 2), pl.ds(pl.multiple_of(row, 16), rows), :].astype(F32)

    for y in range(mesh.sizes["y"]):
        fetch(y).start()
    mesh.greet(mesh.column() + mesh.layer())
    for y in range(mesh.sizes["y"]):
        fetch(y).wait()
    buffers = (source, mine, outgo, income, send_sem, recv_sem, whole_scr)
    for core in range(2):
        pl.when(mesh.core == core)(functools.partial(reduce_blocks, mesh, core, *buffers))

    begin = mesh.me * shard_size - lax.div(mesh.me * shard_size, UNIT) * UNIT
    rows = out_ref.shape[0]
    row, lane = lax.div(begin, 128), lax.rem(begin, 128)
    back = lax.rem(128 - lane, 128)
    first = pltpu.roll(whole_scr[pl.ds(row, rows), :], back, 1)
    second = pltpu.roll(whole_scr[pl.ds(row + 1, rows), :], back, 1)
    at_lane = lax.broadcasted_iota(jnp.int32, (rows, 128), 1)
    place = lax.broadcasted_iota(jnp.int32, (rows, 128), 0) * 128 + at_lane
    total = jnp.where(at_lane < 128 - lane, first, second)
    out_ref[...] = total
    inside = jnp.where(place < shard_size, total, 0.0)
    squares = jnp.sum(jnp.sum(inside * inside, axis=0, keepdims=True), axis=1, keepdims=True)
    lane = lax.broadcasted_iota(jnp.int32, (8, 128), 1)
    row = jnp.where(lane == E, squares, count_ref[...])
    gains = jnp.where(mesh.me == 0, total[0:8, :], 0.0)
    summed = sum_all(mesh, jnp.concatenate([row, gains], axis=0), stats, stat_send, stat_recv)
    total_ref[...] = summed[0:1, :]
    for c in range(D // 128):
        lanes = slice(c * 128, (c + 1) * 128)
        gain_ref[0:1, lanes] = summed[8 + c : 9 + c, :]
        gain_ref[1:2, lanes] = summed[12 + c : 13 + c, :]


def reduce_grads(shards, over, shard_size, window, flat, counts):
    vmem = pl.BlockSpec(memory_space=pltpu.VMEM)
    many = shards * over
    mesh = functools.partial(Mesh3, shards, over)
    pieces = len(pieces_of(window, REDUCE_PIECES))
    steps = over + shards
    units = [(shard_size * d) // UNIT for d in range(many)]
    span = 16 * max(units[d + over - 1] - units[d] for d in range(0, many, over)) + window
    return pl.pallas_call(
        functools.partial(reduce_kernel, mesh, shard_size),
        in_specs=[pl.BlockSpec(memory_space=pl.ANY), vmem],
        out_specs=[vmem] * 3,
        out_shape=[struct((-(-shard_size // 128), 128)), struct((1, 128)), struct((2, D))],
        scratch_shapes=[
            pltpu.VMEM((shards // 2, span, 128), BF16),
            pltpu.VMEM((many // 2, window, 128), BF16),
            pltpu.VMEM((many, window, 128), BF16),
            pltpu.VMEM((window + 16, 128), F32),
            pltpu.VMEM((steps, 16, 128), F32),
            pltpu.SemaphoreType.DMA((shards // 2,)),
            pltpu.SemaphoreType.DMA((many, pieces)),
            pltpu.SemaphoreType.DMA((many, pieces)),
            pltpu.SemaphoreType.DMA((steps,)),
            pltpu.SemaphoreType.DMA((steps,)),
        ],
        compiler_params=pltpu.CompilerParams(
            collective_id=1, has_side_effects=True, vmem_limit_bytes=56 * MIB
        ),
        name="reduce_grads",
    )(flat, counts)


def local_step(flat_rows, tokens, grad_out, routes, segments, weights):
    wall, gain_one, gain_two, wo, w1, w2 = weights
    queries, attended, gates, lse, kv, kvt, start, routes_t, counts = head_forward(
        tokens, routes.T, segments, wall, gain_one
    )
    output, dres, datt, delta, dlogits, flat, extra, dgain_two = middle(
        flat_rows, tokens, grad_out, gain_two, wo, w1, w2, routes_t, gates, attended
    )
    input_grad, flat = head_backward(
        segments, tokens, gain_one, wall, routes_t, start, queries, datt, lse, delta, kv, kvt, dlogits, dres,
        dgain_two, extra, flat,
    )
    return output, input_grad, flat, counts


def per_device(
    shards, over, tokens, grad_out, routes, segments, params, first_moment, second_moment, ema_weights
):
    shard_size = params.shape[0]
    window = window_rows(shard_size, shards * over)
    flat_rows = (shard_size * (shards * over - 1)) // UNIT * 16 + window + 16
    me = lax.axis_index("dp") * over + lax.axis_index("fsdp")
    begin = lax.rem(me * shard_size, UNIT)
    own = lax.dynamic_slice(
        jnp.pad(params, (UNIT, window * 128 - shard_size)), (UNIT - begin,), (window * 128,)
    ).reshape(window, 128)
    wall, gain_one, gain_two, wo, w1, w2 = gather_weights(shards, over, shard_size, own)
    output, input_grad, flat, counts = local_step(
        flat_rows, tokens, grad_out, routes, segments, (wall, gain_one, gain_two, wo, w1, w2)
    )
    reduced, sums, gain_grads = reduce_grads(shards, over, shard_size, window, flat, counts)
    grad_shard = reduced.reshape(-1)[:shard_size]
    total_tokens = tokens.shape[0] * shards * over
    expert_load = sums[0, :E] * (E / (total_tokens * TOPK))
    grad_norm = jnp.sqrt(sums[0, E])
    clipped = grad_shard * (CLIP_LIMIT / jnp.maximum(grad_norm, CLIP_LIMIT))
    new_first = BETA_FIRST * first_moment + (1.0 - BETA_FIRST) * clipped
    new_second = BETA_SECOND * second_moment + (1.0 - BETA_SECOND) * clipped * clipped
    first_hat = new_first / (1.0 - BETA_FIRST**STEP)
    second_hat = new_second / (1.0 - BETA_SECOND**STEP)
    new_params = params * (1.0 - LEARN_RATE * DECAY_RATE) - LEARN_RATE * first_hat / (
        jnp.sqrt(second_hat) + ADAM_EPS
    )
    new_ema = EMA_KEEP * ema_weights + (1.0 - EMA_KEEP) * new_params
    return (
        output,
        input_grad,
        expert_load,
        grad_norm.reshape(1),
        new_params,
        new_first,
        new_second,
        new_ema,
        gain_grads,
    )


def solution(mesh):
    row = P(("dp", "fsdp"), None)
    flat = P(("dp", "fsdp"))
    return jax.shard_map(
        functools.partial(per_device, mesh.shape["dp"], mesh.shape["fsdp"]),
        mesh=mesh,
        in_specs=(row, row, row, row, flat, flat, flat, flat),
        out_specs=(row, row, P(), P(), flat, flat, flat, flat, P()),
        check_vma=False,
    )
```

profile of v0, /device:TPU:0, one launch (start us, length us, event | category | flops | bytes accessed | tf_op | source)
XLA Modules:
  0.0 224.7 jit_solution(8459262301695320700)
XLA Ops:
  0.6 2.0 fusion.own_ref
  2.7 45.6 %gather_weights.1 = (bf16[1696,512]{1,0:T(8,128)(2,1)}, f32[1,512]{1,0:T(1,128)}, f32[1,512]{1,0:T(1,128)}, bf16[1536,512]{1,0:T(8,128)(2,1)}, bf16[512,2048]{1,0:T(8,128)(2,1)}, /*index=5*/bf16[2048,512]{1,0:T(8,128)(2,1)}) custom-call(f32[944,128]{1,0:T(8,128)} %fusion.own_ref), custom_call_target="tpu_custom_call" | custom-call | tf_op jit(solution)/shard_map/gather_weights/pallas_call | solution.py:999
  48.3 24.1 %head_forward.1 = (bf16[512,2048]{1,0:T(8,128)(2,1)}, f32[512,2048]{1,0:T(8,128)}, f32[8,2048]{1,0:T(8,128)}, f32[8,2048]{1,0:T(8,128)}, bf16[2048,128]{1,0:T(8,...) custom-call(s32[2,1024]{1,0:T(2,128)} %segment_smem.3, ...), custom_call_target="tpu_custom_call" | custom-call | flops 10000000000 | bytes 16000000 | tf_op jit(solution)/shard_map/head_forward/pallas_call | solution.py:479
  72.4 54.9 %middle.1 = (bf16[2048,512]{1,0:T(8,128)(2,1)}, f32[2048,512]{1,0:T(8,128)}, bf16[512,2048]{1,0:T(8,128)(2,1)}, f32[8,2048]{1,0:T(8,128)}, f32[24,2048]{1,0:T(8,...) custom-call(bf16[2048,512]{1,0:T(8,128)(2,1)} %x_ref.5, bf16[2048,512]{1,0:T(8,128)(2,1)} %dy_ref.1, ...), custom_call_target="tpu_custom_call" | custom-call | tf_op jit(solution)/shard_map/middle/pallas_call | solution.py:516
  127.3 38.7 %head_backward.1 = (f32[2048,512]{1,0:T(8,128)}, bf16[29328,128]{1,0:T(8,128)(2,1)}) custom-call(s32[2,1024]{1,0:T(2,128)} %segment_smem.3, bf16[2048,512]{1,0:T(8,128)(2,1)} %x_ref.5, f32[1,512]{1,0:T(1,128)} %get-tuple-element.42.gain_ref, bf16[1696,512]{1,0:T(8,128)(2,1)} %get-tuple-element.41.wall_ref, ...), custom_call_target="tpu_custom_call", output_to_operand_aliasing={{1}: (16, {})} | custom-call | flops 30000001024 | bytes 24000000 | tf_op jit(solution)/shard_map/head_backward/pallas_call | solution.py:569
  166.1 0.0 copy-start
  166.1 0.0 copy-start.1
  166.1 0.0 copy-start.2
  166.1 0.0 copy-start.3
  166.1 51.0 %reduce_grads.1 = (f32[916,128]{1,0:T(8,128)}, f32[1,128]{1,0:T(1,128)}, f32[2,512]{1,0:T(2,128)}) custom-call(bf16[29328,128]{1,0:T(8,128)(2,1)} %get-tuple-element.60.flat_ref, f32[1,128]{1,0:T(1,128)} %get-tuple-element.61.count_ref), custom_call_target="tpu_custom_call" | custom-call | tf_op jit(solution)/shard_map/reduce_grads/pallas_call | solution.py:1090
  217.1 1.2 slice.10
  219.1 1.1 multiply_bitcast_fusion
  220.2 0.0 copy-done
  220.2 0.0 copy-done.1
  220.2 0.0 copy-done.2
  220.2 0.0 copy-done.3
  220.2 0.0 copy-start.4
  220.2 2.6 %multiply_add_fusion = (f32[117152]{0:T(1024)}, f32[117152]{0:T(1024)}, f32[117152]{0:T(1024)}, f32[117152]{0:T(1024)}) fusion(f32[117152]{0:T(1024)S(1)} %copy-done.1, f32[117152]{0:T(1024)S(1)} %copy-done, f32[]{:T(128)} %bitcast.5, f32[117248]{0:T(1024)} %bitcast.8, f32[117152]{0:T(1024)S(1)} %copy-done.2, f32[117152]{0:T(1024)S(1)} %copy-done.3), kind=kLoop, calls=%fused_computation.5 | loop fusion | flops 1991584 | bytes 4217476 | tf_op jit(solution)/shard_map/add | solution.py:1157
  222.8 0.0 copy-done.4
  222.8 0.6 copy.20
Async XLA Ops:
  166.1 54.1 %copy-start = (f32[117152]{0:T(1024)S(1)}, f32[117152]{0:T(1024)}, u32[]{:S(2)}) copy-start(f32[117152]{0:T(1024)} %param.12) | copy-start | bytes 1405828
  166.1 54.1 %copy-start.1 = (f32[117152]{0:T(1024)S(1)}, f32[117152]{0:T(1024)}, u32[]{:S(2)}) copy-start(f32[117152]{0:T(1024)} %param.15) | copy-start | bytes 1405828
  166.1 54.1 %copy-start.2 = (f32[117152]{0:T(1024)S(1)}, f32[117152]{0:T(1024)}, u32[]{:S(2)}) copy-start(f32[117152]{0:T(1024)} %param.13) | copy-start | bytes 1405828
  166.1 54.1 %copy-start.3 = (f32[117152]{0:T(1024)S(1)}, f32[117152]{0:T(1024)}, u32[]{:S(2)}) copy-start(f32[117152]{0:T(1024)} %param.14) | copy-start | bytes 1405828
  220.2 2.6 %copy-start.4 = (f32[2,512]{1,0:T(2,128)S(1)}, f32[2,512]{1,0:T(2,128)}, u32[]{:S(2)}) copy-start(f32[2,512]{1,0:T(2,128)} %get-tuple-element.86) | copy-start | bytes 12292
where the time goes:
time: 229 us; the launch traced here: 225 us
  Pallas kernels  214 us (93%)
  local copies, waits for them, and re-layouts  3.83 us (2%)
  other arithmetic  3.7 us (2%)
  between operations  2.83 us (1%)
    pallas_call x1, Pallas kernels, middle(): pl.pallas_call(middle_kernel, grid=(steps,), in_specs=[down(D), down(D),...  54.9 us
    pallas_call x1, Pallas kernels, reduce_grads(): pl.pallas_call(functools.partial(reduce_kernel, mesh, shard_size), in_spe...  51 us
    pallas_call x1, Pallas kernels, gather_weights(): pl.pallas_call(functools.partial(gather_kernel, mesh, shard_size), in_spe...  45.6 us
    pallas_call x1, Pallas kernels, head_backward(): pl.pallas_call(head_backward_kernel, grid=(steps,), in_specs=[SMEM, down(...  38.7 us
    pallas_call x1, Pallas kernels, head_forward(): pl.pallas_call(functools.partial(head_forward_kernel, steps), grid=(steps...  24.1 us

commit v1 on v0

--- a/solution.py
+++ b/solution.py
@@ -247,7 +247,7 @@
 def middle_kernel(
     x_ref, dy_ref, gain_ref, wo_ref, w1_ref, w2_ref, route_ref, gate_ref, att_ref,
     out_ref, dres_ref, datt_ref, delta_ref, dlogit_ref, flat_ref, extra_ref, dgain_ref,
-    slot_scr, head_scr, mix_scr, hidden_scr, dpre_scr, w1t_scr, w2t_scr, dwo_ref, dw1_ref, dw2t_ref, rows_scr, low_scr, row_sem,
+    slot_scr, head_scr, mix_scr, hidden_scr, dpre_scr, dwo_ref, dw1_ref, dw2t_ref, rows_scr, low_scr, row_sem,
 ):
     step = pl.program_id(0)
 
@@ -256,10 +256,6 @@
         dwo_ref[...] = jnp.zeros_like(dwo_ref)
         dw1_ref[...] = jnp.zeros_like(dw1_ref)
         dw2t_ref[...] = jnp.zeros_like(dw2t_ref)
-        for first in range(0, FF, 512):
-            part = slice(first, first + 512)
-            w1t_scr[part, :] = w1_ref[:, part].T
-            w2t_scr[:, part] = w2_ref[part, :].T
         dgain_ref[...] = jnp.zeros_like(dgain_ref)
 
     routes = route_ref[...]
@@ -279,17 +275,17 @@
     second_t = second.T
     dy_t = dy.T
     pre = [nn(second, w1_ref[:, 0:FC])]
-    back = [nn(dy, w2t_scr[:, 0:FC])]
+    back = [nt(dy, w2_ref[0:FC, :])]
     for i in range(FF // FC):
         here = slice(i * FC, (i + 1) * FC)
         if i + 1 < FF // FC:
             after = slice((i + 1) * FC, (i + 2) * FC)
             pre.append(nn(second, w1_ref[:, after]))
-            back.append(nn(dy, w2t_scr[:, after]))
+            back.append(nt(dy, w2_ref[after, :]))
         cdf, density = gelu_parts(pre[i])
         hidden_scr[:, here] = (pre[i] * cdf).astype(BF16)
         dpre_scr[:, here] = (back[i] * (cdf + pre[i] * density)).astype(BF16)
-    dsecond = nn(dpre_scr[...], w1t_scr[...])
+    dsecond = nt(dpre_scr[...], w1_ref[...])
     out_ref[...] = (residual + nn(hidden_scr[...], w2_ref[...])).astype(BF16)
     dw1_ref[...] += nn(second_t, dpre_scr[...])
     dw2t_ref[...] += nn(dy_t, hidden_scr[...])
@@ -540,8 +536,6 @@
             pltpu.VMEM((QW, MB), BF16),
             pltpu.VMEM((MB, FF), BF16),
             pltpu.VMEM((MB, FF), BF16),
-            pltpu.VMEM((FF, D), BF16),
-            pltpu.VMEM((D, FF), BF16),
             pltpu.VMEM((QW, D), F32),
             pltpu.VMEM((D, FF), F32),
             pltpu.VMEM((D, FF), F32),
@@ -775,13 +769,13 @@
     half = mesh.many // 2
     held = {spot: i for i, spot in enumerate(mesh.round_spots())}
 
-    def across(kind, spot):
+    def across(kind, spot, p):
         slot = held[spot]
         return pltpu.make_async_remote_copy(
-            src_ref=source(mesh.number(kind, spot)),
-            dst_ref=income.at[slot],
-            send_sem=send_sem.at[slot, 0],
-            recv_sem=recv_sem.at[slot, 0],
+            src_ref=source(mesh.number(kind, spot), *pieces[p]),
+            dst_ref=income.at[slot, pl.ds(*pieces[p])],
+            send_sem=send_sem.at[slot, p],
+            recv_sem=recv_sem.at[slot, p],
             device_id=mesh.partner,
             device_id_type=MESH,
         )
@@ -802,16 +796,14 @@
         z = {0: 0, 1: 3, 2: 5, 3: 8}.get(spot[2], 2 * spot[2] + 2)
         return z + 2 * (spot[0] > 0) + 2 * (spot[1] > 0)
 
-    for spot in sorted(held, key=far, reverse=True):
-        across(1 - core, spot).start()
     axes = REDUCE_AXES[core]
-    order = sorted(
-        itertools.product(held, range(len(pieces))), key=lambda one: 2 * one[1] / len(pieces) - 2 * far(one[0])
-    )
-    for spot, p in order:
-        if p == 0:
-            across(core, spot).wait_recv()
+
+    def hand(spot, p):
+        across(1 - core, spot, p).start()
+
+    def pass_on(spot, p):
         rows = pl.ds(*pieces[p])
+        across(core, spot, p).wait_recv()
         total = mine(mesh.number(core, spot), *pieces[p]) + income[held[spot], rows].astype(F32)
         last = last_axis(axes, spot)
         for axis in axes[last + 1 :]:
@@ -826,9 +818,14 @@
             outgo[held[spot], rows] = total.astype(BF16)
             step = spot["xyz".index(axes[last])]
             moved(spot, p, mesh.device(core, at(axes[last], step))).start()
-    for spot, p in order:
-        if p == 0:
-            across(1 - core, spot).wait_send()
+
+    every = list(itertools.product(held, range(len(pieces))))
+    events = [(-2 * far(spot) - 4 + 0.01 * p, 0, hand, spot, p) for spot, p in every]
+    events += [(-2 * far(spot) + 2 * p / len(pieces), 1, pass_on, spot, p) for spot, p in every]
+    for _, _, action, spot, p in sorted(events, key=lambda one: one[:2]):
+        action(spot, p)
+    for spot, p in every:
+        across(1 - core, spot, p).wait_send()
         if any(spot):
             moved(spot, p, mesh.partner).wait_send()
 
@@ -1035,8 +1032,9 @@
     window = outgo.shape[1]
     span = part.shape[1]
 
-    def source(owner):
-        return flat_ref.at[pl.ds(first_row(shard_size, owner), window), :]
+    def source(owner, first, rows):
+        row = pl.multiple_of(first_row(shard_size, owner) + first, 16)
+        return flat_ref.at[pl.ds(row, rows), :]
 
     def fetch(y):
         first = first_row(shard_size, (2 * y + mesh.core) * mesh.over)

time: 229 us -> 228 us (level)
  no operation moved by 1% of the time
where the time goes in v1:
time: 228 us; the launch traced here: 224 us
  Pallas kernels  214 us (94%)
  local copies, waits for them, and re-layouts  3.83 us (2%)
  other arithmetic  3.7 us (2%)
  between operations  2.83 us (1%)
    pallas_call x1, Pallas kernels, middle(): pl.pallas_call(middle_kernel, grid=(steps,), in_specs=[down(D), down(D),...  53.4 us
    pallas_call x1, Pallas kernels, reduce_grads(): pl.pallas_call(functools.partial(reduce_kernel, mesh, shard_size), in_spe...  50.1 us
    pallas_call x1, Pallas kernels, gather_weights(): pl.pallas_call(functools.partial(gather_kernel, mesh, shard_size), in_spe...  45.6 us
    pallas_call x1, Pallas kernels, head_backward(): pl.pallas_call(head_backward_kernel, grid=(steps,), in_specs=[SMEM, down(...  39.9 us
    pallas_call x1, Pallas kernels, head_forward(): pl.pallas_call(functools.partial(head_forward_kernel, steps), grid=(steps...  24.9 us

profile of v1, /device:TPU:0, one launch (start us, length us, event | category | flops | bytes accessed | tf_op | source)
XLA Modules:
  0.0 224.3 jit_solution(14508706247847997051)
XLA Ops:
  0.6 2.0 fusion.own_ref
  2.7 45.6 %gather_weights.1 = (bf16[1696,512]{1,0:T(8,128)(2,1)}, f32[1,512]{1,0:T(1,128)}, f32[1,512]{1,0:T(1,128)}, bf16[1536,512]{1,0:T(8,128)(2,1)}, bf16[512,2048]{1,0:T(8,128)(2,1)}, /*index=5*/bf16[2048,512]{1,0:T(8,128)(2,1)}) custom-call(f32[944,128]{1,0:T(8,128)} %fusion.own_ref), custom_call_target="tpu_custom_call" | custom-call | tf_op jit(solution)/shard_map/gather_weights/pallas_call | solution.py:996
  48.3 24.9 %head_forward.1 = (bf16[512,2048]{1,0:T(8,128)(2,1)}, f32[512,2048]{1,0:T(8,128)}, f32[8,2048]{1,0:T(8,128)}, f32[8,2048]{1,0:T(8,128)}, bf16[2048,128]{1,0:T(8,...) custom-call(s32[2,1024]{1,0:T(2,128)} %segment_smem.3, ...), custom_call_target="tpu_custom_call" | custom-call | flops 10000000000 | bytes 16000000 | tf_op jit(solution)/shard_map/head_forward/pallas_call | solution.py:475
  73.2 53.4 %middle.1 = (bf16[2048,512]{1,0:T(8,128)(2,1)}, f32[2048,512]{1,0:T(8,128)}, bf16[512,2048]{1,0:T(8,128)(2,1)}, f32[8,2048]{1,0:T(8,128)}, f32[24,2048]{1,0:T(8,...) custom-call(bf16[2048,512]{1,0:T(8,128)(2,1)} %x_ref.5, bf16[2048,512]{1,0:T(8,128)(2,1)} %dy_ref.1, ...), custom_call_target="tpu_custom_call" | custom-call | tf_op jit(solution)/shard_map/middle/pallas_call | solution.py:512
  126.6 39.9 %head_backward.1 = (f32[2048,512]{1,0:T(8,128)}, bf16[29328,128]{1,0:T(8,128)(2,1)}) custom-call(s32[2,1024]{1,0:T(2,128)} %segment_smem.3, bf16[2048,512]{1,0:T(8,128)(2,1)} %x_ref.5, f32[1,512]{1,0:T(1,128)} %get-tuple-element.42.gain_ref, bf16[1696,512]{1,0:T(8,128)(2,1)} %get-tuple-element.41.wall_ref, ...), custom_call_target="tpu_custom_call", output_to_operand_aliasing={{1}: (16, {})} | custom-call | flops 30000001024 | bytes 24000000 | tf_op jit(solution)/shard_map/head_backward/pallas_call | solution.py:563
  166.5 0.0 copy-start
  166.6 0.0 copy-start.1
  166.6 0.0 copy-start.2
  166.6 0.0 copy-start.3
  166.6 50.1 %reduce_grads.1 = (f32[916,128]{1,0:T(8,128)}, f32[1,128]{1,0:T(1,128)}, f32[2,512]{1,0:T(2,128)}) custom-call(bf16[29328,128]{1,0:T(8,128)(2,1)} %get-tuple-element.60.flat_ref, f32[1,128]{1,0:T(1,128)} %get-tuple-element.61.count_ref), custom_call_target="tpu_custom_call" | custom-call | tf_op jit(solution)/shard_map/reduce_grads/pallas_call | solution.py:1088
  216.7 1.2 slice.10
  218.6 1.1 multiply_bitcast_fusion
  219.8 0.0 copy-done
  219.8 0.0 copy-done.1
  219.8 0.0 copy-done.2
  219.8 0.0 copy-done.3
  219.8 0.0 copy-start.4
  219.8 2.6 %multiply_add_fusion = (f32[117152]{0:T(1024)}, f32[117152]{0:T(1024)}, f32[117152]{0:T(1024)}, f32[117152]{0:T(1024)}) fusion(f32[117152]{0:T(1024)S(1)} %copy-done.1, f32[117152]{0:T(1024)S(1)} %copy-done, f32[]{:T(128)} %bitcast.5, f32[117248]{0:T(1024)} %bitcast.8, f32[117152]{0:T(1024)S(1)} %copy-done.2, f32[117152]{0:T(1024)S(1)} %copy-done.3), kind=kLoop, calls=%fused_computation.5 | loop fusion | flops 1991584 | bytes 4217476 | tf_op jit(solution)/shard_map/add | solution.py:1155
  222.4 0.0 copy-done.4
  222.4 0.6 copy.20
Async XLA Ops:
  166.5 53.2 %copy-start = (f32[117152]{0:T(1024)S(1)}, f32[117152]{0:T(1024)}, u32[]{:S(2)}) copy-start(f32[117152]{0:T(1024)} %param.12) | copy-start | bytes 1405828
  166.6 53.2 %copy-start.1 = (f32[117152]{0:T(1024)S(1)}, f32[117152]{0:T(1024)}, u32[]{:S(2)}) copy-start(f32[117152]{0:T(1024)} %param.15) | copy-start | bytes 1405828
  166.6 53.2 %copy-start.2 = (f32[117152]{0:T(1024)S(1)}, f32[117152]{0:T(1024)}, u32[]{:S(2)}) copy-start(f32[117152]{0:T(1024)} %param.13) | copy-start | bytes 1405828
  166.6 53.2 %copy-start.3 = (f32[117152]{0:T(1024)S(1)}, f32[117152]{0:T(1024)}, u32[]{:S(2)}) copy-start(f32[117152]{0:T(1024)} %param.14) | copy-start | bytes 1405828
  219.8 2.6 %copy-start.4 = (f32[2,512]{1,0:T(2,128)S(1)}, f32[2,512]{1,0:T(2,128)}, u32[]{:S(2)}) copy-start(f32[2,512]{1,0:T(2,128)} %get-tuple-element.86) | copy-start | bytes 12292

commit v2 on v1

--- a/solution.py
+++ b/solution.py
@@ -245,14 +245,21 @@
 
 
 def middle_kernel(
-    x_ref, dy_ref, gain_ref, wo_ref, w1_ref, w2_ref, route_ref, gate_ref, att_ref,
+    x_ref, dy_ref, gain_ref, wo_hbm, w1_hbm, w2_hbm, route_ref, gate_ref, att_ref,
     out_ref, dres_ref, datt_ref, delta_ref, dlogit_ref, flat_ref, extra_ref, dgain_ref,
     slot_scr, head_scr, mix_scr, hidden_scr, dpre_scr, dwo_ref, dw1_ref, dw2t_ref, rows_scr, low_scr, row_sem,
+    wo_ref, w1_ref, w2_ref, weight_sem,
 ):
     step = pl.program_id(0)
+    weights = [
+        pltpu.make_async_copy(source, target, weight_sem.at[i])
+        for i, (source, target) in enumerate(((wo_hbm, wo_ref), (w2_hbm, w2_ref), (w1_hbm, w1_ref)))
+    ]
 
     @pl.when(step == 0)
     def _():
+        for copy in weights:
+            copy.start()
         dwo_ref[...] = jnp.zeros_like(dwo_ref)
         dw1_ref[...] = jnp.zeros_like(dw1_ref)
         dw2t_ref[...] = jnp.zeros_like(dw2t_ref)
@@ -268,6 +275,12 @@
     x = x_ref[...].astype(F32)
     dy = dy_ref[...]
     mixed = mix_scr[...]
+
+    @pl.when(step == 0)
+    def _():
+        for copy in weights:
+            copy.wait()
+
     residual = x + tn(mixed, wo_ref[...])
     scale = rms_scale(residual)
     gain = gain_ref[...]
@@ -457,6 +470,7 @@
 
 
 SMEM = pl.BlockSpec(memory_space=pltpu.SMEM)
+HBM = pl.BlockSpec(memory_space=pl.ANY)
 
 
 def struct(shape, kind=F32):
@@ -513,8 +527,7 @@
         middle_kernel,
         grid=(steps,),
         in_specs=[
-            down(D), down(D), whole((1, D)), whole((QW, D)), whole((D, FF)), whole((FF, D)),
-            across(TOPK), across(TOPK), across(TOPK * H),
+            down(D), down(D), whole((1, D)), HBM, HBM, HBM, across(TOPK), across(TOPK), across(TOPK * H),
         ],
         out_specs=[
             down(D), down(D), across(TOPK * H), across(TOPK), across(E),
@@ -541,6 +554,10 @@
             pltpu.VMEM((D, FF), F32),
             pltpu.VMEM((flat_rows - WO_ROW, 128), F32),
             pltpu.VMEM((flat_rows - WO_ROW - 8, 128), BF16),
+            pltpu.SemaphoreType.DMA((3,)),
+            pltpu.VMEM((QW, D), BF16),
+            pltpu.VMEM((D, FF), BF16),
+            pltpu.VMEM((FF, D), BF16),
             pltpu.SemaphoreType.DMA((3,)),
         ],
         compiler_params=params_for(60),
@@ -764,7 +781,7 @@
     lax.fori_loop(0, mesh.many // 2, one, 0)
 
 
-def reduce_blocks(mesh, core, source, mine, outgo, income, send_sem, recv_sem, total_ref):
+def reduce_blocks(mesh, core, source, mine, outgo, income, send_sem, recv_sem, total_ref, closing):
     pieces = pieces_of(outgo.shape[1], REDUCE_PIECES)
     half = mesh.many // 2
     held = {spot: i for i, spot in enumerate(mesh.round_spots())}
@@ -823,14 +840,15 @@
     events = [(-2 * far(spot) - 4 + 0.01 * p, 0, hand, spot, p) for spot, p in every]
     events += [(-2 * far(spot) + 2 * p / len(pieces), 1, pass_on, spot, p) for spot, p in every]
     for _, _, action, spot, p in sorted(events, key=lambda one: one[:2]):
-        action(spot, p)
-    for spot, p in every:
+        if not closing:
+            action(spot, p)
+    for spot, p in every if closing else ():
         across(1 - core, spot, p).wait_send()
         if any(spot):
             moved(spot, p, mesh.partner).wait_send()
 
 
-def sum_all(mesh, mine, stats, send_sem, recv_sem):
+def sum_all(mesh, mine, stats, send_sem, recv_sem, meanwhile):
     column = mesh.sizes["z"] * 2
     layer = mesh.sizes["x"] * mesh.sizes["y"]
     groups = (
@@ -863,6 +881,8 @@
 
         for j, device in enumerate(devices):
             sent(j, device).start()
+        if not base:
+            meanwhile()
         for j in range(1, size):
             come(lax.rem(here + j, size)).wait_recv()
         for j, device in enumerate(devices):
@@ -942,14 +962,22 @@
 ):
     mesh = mesh()
     many = mesh.many
+    window = land.shape[1]
+    begin = mesh.me * shard_size - lax.div(mesh.me * shard_size, UNIT) * UNIT
+    row, lane = lax.div(begin, 128), lax.rem(begin, 128)
+    flat[0 : window + 48, :] = jnp.zeros((window + 48, 128), F32)
+    flat[24 : 24 + own_ref.shape[0], :] = own_ref[...]
+    first = pltpu.roll(flat[pl.ds(24 - row, window), :], lane, 1)
+    second = pltpu.roll(flat[pl.ds(23 - row, window), :], lane, 1)
+    at_lane = lax.broadcasted_iota(jnp.int32, (window, 128), 1)
+    land[mesh.me] = jnp.where(at_lane >= lane, first, second).astype(BF16)
     mesh.greet(mesh.near())
-    land[mesh.me] = own_ref[...].astype(BF16)
     gather_blocks(mesh, land, send_sem, recv_sem, True)
     each_owner(mesh, mesh.core, functools.partial(lay_inner, shard_size, many, land, flat))
 
     def arrive(owner):
         for p in range(recv_sem.shape[1]):
-            rows = pl.ds(*pieces_of(own_ref.shape[0])[p])
+            rows = pl.ds(*pieces_of(window)[p])
             pltpu.make_async_remote_copy(
                 src_ref=land.at[owner, rows],
                 dst_ref=land.at[owner, rows],
@@ -985,8 +1013,7 @@
         one.wait()
 
 
-def gather_weights(shards, over, shard_size, own):
-    window = own.shape[0]
+def gather_weights(shards, over, shard_size, window, own):
     many = shards * over
     rows = (shard_size * (many - 1)) // UNIT * 16 + window
     vmem = pl.BlockSpec(memory_space=pltpu.VMEM)
@@ -1051,8 +1078,14 @@
     for y in range(mesh.sizes["y"]):
         fetch(y).wait()
     buffers = (source, mine, outgo, income, send_sem, recv_sem, whole_scr)
-    for core in range(2):
-        pl.when(mesh.core == core)(functools.partial(reduce_blocks, mesh, core, *buffers))
+
+    def reduce_all(closing):
+        for core in range(2):
+            pl.when(mesh.core == core)(
+                functools.partial(reduce_blocks, mesh, core, *buffers, closing=closing)
+            )
+
+    reduce_all(False)
 
     begin = mesh.me * shard_size - lax.div(mesh.me * shard_size, UNIT) * UNIT
     rows = out_ref.shape[0]
@@ -1069,7 +1102,10 @@
     lane = lax.broadcasted_iota(jnp.int32, (8, 128), 1)
     row = jnp.where(lane == E, squares, count_ref[...])
     gains = jnp.where(mesh.me == 0, total[0:8, :], 0.0)
-    summed = sum_all(mesh, jnp.concatenate([row, gains], axis=0), stats, stat_send, stat_recv)
+    summed = sum_all(
+        mesh, jnp.concatenate([row, gains], axis=0), stats, stat_send, stat_recv,
+        lambda: reduce_all(True),
+    )
     total_ref[...] = summed[0:1, :]
     for c in range(D // 128):
         lanes = slice(c * 128, (c + 1) * 128)
@@ -1130,12 +1166,9 @@
     shard_size = params.shape[0]
     window = window_rows(shard_size, shards * over)
     flat_rows = (shard_size * (shards * over - 1)) // UNIT * 16 + window + 16
-    me = lax.axis_index("dp") * over + lax.axis_index("fsdp")
-    begin = lax.rem(me * shard_size, UNIT)
-    own = lax.dynamic_slice(
-        jnp.pad(params, (UNIT, window * 128 - shard_size)), (UNIT - begin,), (window * 128,)
-    ).reshape(window, 128)
-    wall, gain_one, gain_two, wo, w1, w2 = gather_weights(shards, over, shard_size, own)
+    own_rows = -(-shard_size // 1024) * 8
+    own = jnp.pad(params, (0, own_rows * 128 - shard_size)).reshape(own_rows, 128)
+    wall, gain_one, gain_two, wo, w1, w2 = gather_weights(shards, over, shard_size, window, own)
     output, input_grad, flat, counts = local_step(
         flat_rows, tokens, grad_out, routes, segments, (wall, gain_one, gain_two, wo, w1, w2)
     )

time: 228 us -> 230 us (level)
    pallas_call x1, Pallas kernels: 50.1 us -> 52.9 us  [reduce_grads(): pl.pallas_call(functools.partial(reduce_kernel, mesh, shard_size), in_spe...]
where the time goes in v2:
time: 230 us; the launch traced here: 226 us
  Pallas kernels  216 us (94%)
  other arithmetic  3.7 us (2%)
  local copies, waits for them, and re-layouts  3.64 us (2%)
  between operations  2.82 us (1%)
    pallas_call x1, Pallas kernels, middle(): pl.pallas_call(middle_kernel, grid=(steps,), in_specs=[down(D), down(D),...  55.2 us
    pallas_call x1, Pallas kernels, reduce_grads(): pl.pallas_call(functools.partial(reduce_kernel, mesh, shard_size), in_spe...  52.9 us
    pallas_call x1, Pallas kernels, gather_weights(): pl.pallas_call(functools.partial(gather_kernel, mesh, shard_size), in_spe...  45.8 us
    pallas_call x1, Pallas kernels, head_backward(): pl.pallas_call(head_backward_kernel, grid=(steps,), in_specs=[SMEM, down(...  38.1 us
    pallas_call x1, Pallas kernels, head_forward(): pl.pallas_call(functools.partial(head_forward_kernel, steps), grid=(steps...  23.7 us

profile of v2, /device:TPU:0, one launch (start us, length us, event | category | flops | bytes accessed | tf_op | source)
XLA Modules:
  0.0 225.9 jit_solution(4370191485400901186)
XLA Ops:
  0.6 1.8 pad_bitcast_fusion.own_ref
  2.5 45.8 %gather_weights.1 = (bf16[1696,512]{1,0:T(8,128)(2,1)}, f32[1,512]{1,0:T(1,128)}, f32[1,512]{1,0:T(1,128)}, bf16[1536,512]{1,0:T(8,128)(2,1)}, bf16[512,2048]{1,0:T(8,128)(2,1)}, /*index=5*/bf16[2048,512]{1,0:T(8,128)(2,1)}) custom-call(f32[920,128]{1,0:T(8,128)} %pad_bitcast_fusion.own_ref), custom_call_target="tpu_custom_call" | custom-call | tf_op jit(solution)/shard_map/gather_weights/pallas_call | solution.py:1023
  48.2 23.7 %head_forward.1 = (bf16[512,2048]{1,0:T(8,128)(2,1)}, f32[512,2048]{1,0:T(8,128)}, f32[8,2048]{1,0:T(8,128)}, f32[8,2048]{1,0:T(8,128)}, bf16[2048,128]{1,0:T(8,...) custom-call(s32[2,1024]{1,0:T(2,128)} %segment_smem.3, ...), custom_call_target="tpu_custom_call" | custom-call | flops 10000000000 | bytes 16000000 | tf_op jit(solution)/shard_map/head_forward/pallas_call | solution.py:489
  72.0 55.2 %middle.1 = (bf16[2048,512]{1,0:T(8,128)(2,1)}, f32[2048,512]{1,0:T(8,128)}, bf16[512,2048]{1,0:T(8,128)(2,1)}, f32[8,2048]{1,0:T(8,128)}, f32[24,2048]{1,0:T(8,...) custom-call(bf16[2048,512]{1,0:T(8,128)(2,1)} %x_ref.5, bf16[2048,512]{1,0:T(8,128)(2,1)} %dy_ref.1, ...), custom_call_target="tpu_custom_call" | custom-call | tf_op jit(solution)/shard_map/middle/pallas_call | solution.py:526
  127.2 38.1 %head_backward.1 = (f32[2048,512]{1,0:T(8,128)}, bf16[29328,128]{1,0:T(8,128)(2,1)}) custom-call(s32[2,1024]{1,0:T(2,128)} %segment_smem.3, bf16[2048,512]{1,0:T(8,128)(2,1)} %x_ref.5, f32[1,512]{1,0:T(1,128)} %get-tuple-element.42.gain_ref, bf16[1696,512]{1,0:T(8,128)(2,1)} %get-tuple-element.41.wall_ref, ...), custom_call_target="tpu_custom_call", output_to_operand_aliasing={{1}: (16, {})} | custom-call | flops 30000001024 | bytes 24000000 | tf_op jit(solution)/shard_map/head_backward/pallas_call | solution.py:580
  165.4 0.0 copy-start
  165.4 0.0 copy-start.1
  165.4 0.0 copy-start.2
  165.4 0.0 copy-start.3
  165.4 52.9 %reduce_grads.1 = (f32[916,128]{1,0:T(8,128)}, f32[1,128]{1,0:T(1,128)}, f32[2,512]{1,0:T(2,128)}) custom-call(bf16[29328,128]{1,0:T(8,128)(2,1)} %get-tuple-element.60.flat_ref, f32[1,128]{1,0:T(1,128)} %get-tuple-element.61.count_ref), custom_call_target="tpu_custom_call" | custom-call | tf_op jit(solution)/shard_map/reduce_grads/pallas_call | solution.py:1124
  218.3 1.2 slice.10
  220.2 1.1 multiply_bitcast_fusion
  221.3 0.0 copy-done
  221.3 0.0 copy-done.1
  221.4 0.0 copy-done.2
  221.4 0.0 copy-done.3
  221.4 0.0 copy-start.4
  221.4 2.6 %multiply_add_fusion = (f32[117152]{0:T(1024)}, f32[117152]{0:T(1024)}, f32[117152]{0:T(1024)}, f32[117152]{0:T(1024)}) fusion(f32[117152]{0:T(1024)S(1)} %copy-done.1, f32[117152]{0:T(1024)S(1)} %copy-done, f32[]{:T(128)} %bitcast.5, f32[117248]{0:T(1024)} %bitcast.8, f32[117152]{0:T(1024)S(1)} %copy-done.2, f32[117152]{0:T(1024)S(1)} %copy-done.3), kind=kLoop, calls=%fused_computation.3 | loop fusion | flops 1991584 | bytes 4217476 | tf_op jit(solution)/shard_map/add | solution.py:1188
  224.0 0.0 copy-done.4
  224.0 0.6 copy.20
Async XLA Ops:
  165.4 56.0 %copy-start = (f32[117152]{0:T(1024)S(1)}, f32[117152]{0:T(1024)}, u32[]{:S(2)}) copy-start(f32[117152]{0:T(1024)} %param.12) | copy-start | bytes 1405828
  165.4 56.0 %copy-start.1 = (f32[117152]{0:T(1024)S(1)}, f32[117152]{0:T(1024)}, u32[]{:S(2)}) copy-start(f32[117152]{0:T(1024)} %param.15) | copy-start | bytes 1405828
  165.4 56.0 %copy-start.2 = (f32[117152]{0:T(1024)S(1)}, f32[117152]{0:T(1024)}, u32[]{:S(2)}) copy-start(f32[117152]{0:T(1024)} %param.13) | copy-start | bytes 1405828
  165.4 56.0 %copy-start.3 = (f32[117152]{0:T(1024)S(1)}, f32[117152]{0:T(1024)}, u32[]{:S(2)}) copy-start(f32[117152]{0:T(1024)} %param.14) | copy-start | bytes 1405828
  221.4 2.6 %copy-start.4 = (f32[2,512]{1,0:T(2,128)S(1)}, f32[2,512]{1,0:T(2,128)}, u32[]{:S(2)}) copy-start(f32[2,512]{1,0:T(2,128)} %get-tuple-element.86) | copy-start | bytes 12292

commit v3 on v2

--- a/solution.py
+++ b/solution.py
@@ -245,21 +245,14 @@
 
 
 def middle_kernel(
-    x_ref, dy_ref, gain_ref, wo_hbm, w1_hbm, w2_hbm, route_ref, gate_ref, att_ref,
+    x_ref, dy_ref, gain_ref, wo_ref, w1_ref, w2_ref, route_ref, gate_ref, att_ref,
     out_ref, dres_ref, datt_ref, delta_ref, dlogit_ref, flat_ref, extra_ref, dgain_ref,
     slot_scr, head_scr, mix_scr, hidden_scr, dpre_scr, dwo_ref, dw1_ref, dw2t_ref, rows_scr, low_scr, row_sem,
-    wo_ref, w1_ref, w2_ref, weight_sem,
 ):
     step = pl.program_id(0)
-    weights = [
-        pltpu.make_async_copy(source, target, weight_sem.at[i])
-        for i, (source, target) in enumerate(((wo_hbm, wo_ref), (w2_hbm, w2_ref), (w1_hbm, w1_ref)))
-    ]
 
     @pl.when(step == 0)
     def _():
-        for copy in weights:
-            copy.start()
         dwo_ref[...] = jnp.zeros_like(dwo_ref)
         dw1_ref[...] = jnp.zeros_like(dw1_ref)
         dw2t_ref[...] = jnp.zeros_like(dw2t_ref)
@@ -275,12 +268,6 @@
     x = x_ref[...].astype(F32)
     dy = dy_ref[...]
     mixed = mix_scr[...]
-
-    @pl.when(step == 0)
-    def _():
-        for copy in weights:
-            copy.wait()
-
     residual = x + tn(mixed, wo_ref[...])
     scale = rms_scale(residual)
     gain = gain_ref[...]
@@ -470,7 +457,6 @@
 
 
 SMEM = pl.BlockSpec(memory_space=pltpu.SMEM)
-HBM = pl.BlockSpec(memory_space=pl.ANY)
 
 
 def struct(shape, kind=F32):
@@ -527,7 +513,8 @@
         middle_kernel,
         grid=(steps,),
         in_specs=[
-            down(D), down(D), whole((1, D)), HBM, HBM, HBM, across(TOPK), across(TOPK), across(TOPK * H),
+            down(D), down(D), whole((1, D)), whole((QW, D)), whole((D, FF)), whole((FF, D)),
+            across(TOPK), across(TOPK), across(TOPK * H),
         ],
         out_specs=[
             down(D), down(D), across(TOPK * H), across(TOPK), across(E),
@@ -554,10 +541,6 @@
             pltpu.VMEM((D, FF), F32),
             pltpu.VMEM((flat_rows - WO_ROW, 128), F32),
             pltpu.VMEM((flat_rows - WO_ROW - 8, 128), BF16),
-            pltpu.SemaphoreType.DMA((3,)),
-            pltpu.VMEM((QW, D), BF16),
-            pltpu.VMEM((D, FF), BF16),
-            pltpu.VMEM((FF, D), BF16),
             pltpu.SemaphoreType.DMA((3,)),
         ],
         compiler_params=params_for(60),
@@ -697,7 +680,7 @@
 
 
 GATHER_AXES = (("zxy", "yzx"), ("zyx", "xzy"))
-REDUCE_PIECES = 3
+REDUCE_PIECES = 2
 REDUCE_AXES = ("zxy", "zyx")
 
 

time: 230 us -> 228 us (level)
    pallas_call x1, Pallas kernels: 52.9 us -> 48.5 us  [reduce_grads(): pl.pallas_call(functools.partial(reduce_kernel, mesh, shard_size), in_spe...]
    pallas_call x1, Pallas kernels: 38.1 us -> 41.4 us  [head_backward(): pl.pallas_call(head_backward_kernel, grid=(steps,), in_specs=[SMEM, down(...]
where the time goes in v3:
time: 228 us; the launch traced here: 225 us
  Pallas kernels  215 us (94%)
  other arithmetic  3.7 us (2%)
  local copies, waits for them, and re-layouts  3.64 us (2%)
  between operations  2.82 us (1%)
    pallas_call x1, Pallas kernels, middle(): pl.pallas_call(middle_kernel, grid=(steps,), in_specs=[down(D), down(D),...  53.4 us
    pallas_call x1, Pallas kernels, reduce_grads(): pl.pallas_call(functools.partial(reduce_kernel, mesh, shard_size), in_spe...  48.5 us
    pallas_call x1, Pallas kernels, gather_weights(): pl.pallas_call(functools.partial(gather_kernel, mesh, shard_size), in_spe...  45.8 us
    pallas_call x1, Pallas kernels, head_backward(): pl.pallas_call(head_backward_kernel, grid=(steps,), in_specs=[SMEM, down(...  41.4 us
    pallas_call x1, Pallas kernels, head_forward(): pl.pallas_call(functools.partial(head_forward_kernel, steps), grid=(steps...  25.7 us

profile of v3, /device:TPU:0, one launch (start us, length us, event | category | flops | bytes accessed | tf_op | source)
XLA Modules:
  0.0 224.9 jit_solution(12836138316101158080)
XLA Ops:
  0.6 1.8 pad_bitcast_fusion.own_ref
  2.5 45.8 %gather_weights.1 = (bf16[1696,512]{1,0:T(8,128)(2,1)}, f32[1,512]{1,0:T(1,128)}, f32[1,512]{1,0:T(1,128)}, bf16[1536,512]{1,0:T(8,128)(2,1)}, bf16[512,2048]{1,0:T(8,128)(2,1)}, /*index=5*/bf16[2048,512]{1,0:T(8,128)(2,1)}) custom-call(f32[920,128]{1,0:T(8,128)} %pad_bitcast_fusion.own_ref), custom_call_target="tpu_custom_call" | custom-call | tf_op jit(solution)/shard_map/gather_weights/pallas_call | solution.py:1006
  48.2 25.7 %head_forward.1 = (bf16[512,2048]{1,0:T(8,128)(2,1)}, f32[512,2048]{1,0:T(8,128)}, f32[8,2048]{1,0:T(8,128)}, f32[8,2048]{1,0:T(8,128)}, bf16[2048,128]{1,0:T(8,...) custom-call(s32[2,1024]{1,0:T(2,128)} %segment_smem.3, ...), custom_call_target="tpu_custom_call" | custom-call | flops 10000000000 | bytes 16000000 | tf_op jit(solution)/shard_map/head_forward/pallas_call | solution.py:475
  74.0 53.4 %middle.1 = (bf16[2048,512]{1,0:T(8,128)(2,1)}, f32[2048,512]{1,0:T(8,128)}, bf16[512,2048]{1,0:T(8,128)(2,1)}, f32[8,2048]{1,0:T(8,128)}, f32[24,2048]{1,0:T(8,...) custom-call(bf16[2048,512]{1,0:T(8,128)(2,1)} %x_ref.5, bf16[2048,512]{1,0:T(8,128)(2,1)} %dy_ref.1, ...), custom_call_target="tpu_custom_call" | custom-call | tf_op jit(solution)/shard_map/middle/pallas_call | solution.py:512
  127.4 41.4 %head_backward.1 = (f32[2048,512]{1,0:T(8,128)}, bf16[29328,128]{1,0:T(8,128)(2,1)}) custom-call(s32[2,1024]{1,0:T(2,128)} %segment_smem.3, bf16[2048,512]{1,0:T(8,128)(2,1)} %x_ref.5, f32[1,512]{1,0:T(1,128)} %get-tuple-element.42.gain_ref, bf16[1696,512]{1,0:T(8,128)(2,1)} %get-tuple-element.41.wall_ref, ...), custom_call_target="tpu_custom_call", output_to_operand_aliasing={{1}: (16, {})} | custom-call | flops 30000001024 | bytes 24000000 | tf_op jit(solution)/shard_map/head_backward/pallas_call | solution.py:563
  168.8 0.0 copy-start
  168.8 0.0 copy-start.1
  168.8 0.0 copy-start.2
  168.8 0.0 copy-start.3
  168.8 48.5 %reduce_grads.1 = (f32[916,128]{1,0:T(8,128)}, f32[1,128]{1,0:T(1,128)}, f32[2,512]{1,0:T(2,128)}) custom-call(bf16[29328,128]{1,0:T(8,128)(2,1)} %get-tuple-element.60.flat_ref, f32[1,128]{1,0:T(1,128)} %get-tuple-element.61.count_ref), custom_call_target="tpu_custom_call" | custom-call | tf_op jit(solution)/shard_map/reduce_grads/pallas_call | solution.py:1107
  217.3 1.2 slice.10
  219.3 1.1 multiply_bitcast_fusion
  220.4 0.0 copy-done
  220.4 0.0 copy-done.1
  220.4 0.0 copy-done.2
  220.4 0.0 copy-done.3
  220.4 0.0 copy-start.4
  220.4 2.6 %multiply_add_fusion = (f32[117152]{0:T(1024)}, f32[117152]{0:T(1024)}, f32[117152]{0:T(1024)}, f32[117152]{0:T(1024)}) fusion(f32[117152]{0:T(1024)S(1)} %copy-done.1, f32[117152]{0:T(1024)S(1)} %copy-done, f32[]{:T(128)} %bitcast.5, f32[117248]{0:T(1024)} %bitcast.8, f32[117152]{0:T(1024)S(1)} %copy-done.2, f32[117152]{0:T(1024)S(1)} %copy-done.3), kind=kLoop, calls=%fused_computation.3 | loop fusion | flops 1991584 | bytes 4217476 | tf_op jit(solution)/shard_map/add | solution.py:1171
  223.0 0.0 copy-done.4
  223.0 0.6 copy.20
Async XLA Ops:
  168.8 51.6 %copy-start = (f32[117152]{0:T(1024)S(1)}, f32[117152]{0:T(1024)}, u32[]{:S(2)}) copy-start(f32[117152]{0:T(1024)} %param.12) | copy-start | bytes 1405828
  168.8 51.6 %copy-start.1 = (f32[117152]{0:T(1024)S(1)}, f32[117152]{0:T(1024)}, u32[]{:S(2)}) copy-start(f32[117152]{0:T(1024)} %param.15) | copy-start | bytes 1405828
  168.8 51.6 %copy-start.2 = (f32[117152]{0:T(1024)S(1)}, f32[117152]{0:T(1024)}, u32[]{:S(2)}) copy-start(f32[117152]{0:T(1024)} %param.13) | copy-start | bytes 1405828
  168.8 51.6 %copy-start.3 = (f32[117152]{0:T(1024)S(1)}, f32[117152]{0:T(1024)}, u32[]{:S(2)}) copy-start(f32[117152]{0:T(1024)} %param.14) | copy-start | bytes 1405828
  220.4 2.6 %copy-start.4 = (f32[2,512]{1,0:T(2,128)S(1)}, f32[2,512]{1,0:T(2,128)}, u32[]{:S(2)}) copy-start(f32[2,512]{1,0:T(2,128)} %get-tuple-element.86) | copy-start | bytes 12292

commit v4 on v3

--- a/solution.py
+++ b/solution.py
@@ -665,7 +665,7 @@
     return max([i for i, axis in enumerate(axes) if spot["xyz".index(axis)]], default=-1)
 
 
-def pieces_of(window, count=2):
+def pieces_of(window, count=3):
     if window < 512:
         return [(0, window)]
     ends = [window // 16 * i // count * 16 for i in range(count)] + [window]
@@ -721,7 +721,7 @@
         turn = 0.5 * abs(spot[2]) + (spot[0] > 0) + (spot[1] > 0) + (0.001 if spot[2] < 0 else 0)
         for p in range(len(pieces)):
             sends = []
-            for axis, step in onward(mesh, GATHER_AXES[core][p], spot):
+            for axis, step in onward(mesh, GATHER_AXES[core][p % 2], spot):
                 key = (spot[0], spot[1], spot[2] % mesh.sizes["z"], axis, step)
                 away = mesh.exists(step) if axis == "z" else True
                 if away is not False:

time: 228 us -> 230 us (level)
    pallas_call x1, Pallas kernels: 45.8 us -> 48.5 us  [gather_weights(): pl.pallas_call(functools.partial(gather_kernel, mesh, shard_size), in_spe...]
where the time goes in v4:
time: 230 us; the launch traced here: 225 us
  Pallas kernels  215 us (93%)
  other arithmetic  3.7 us (2%)
  local copies, waits for them, and re-layouts  3.64 us (2%)
  between operations  2.82 us (1%)
    pallas_call x1, Pallas kernels, middle(): pl.pallas_call(middle_kernel, grid=(steps,), in_specs=[down(D), down(D),...  53.4 us
    pallas_call x1, Pallas kernels, reduce_grads(): pl.pallas_call(functools.partial(reduce_kernel, mesh, shard_size), in_spe...  49.3 us
    pallas_call x1, Pallas kernels, gather_weights(): pl.pallas_call(functools.partial(gather_kernel, mesh, shard_size), in_spe...  48.5 us
    pallas_call x1, Pallas kernels, head_backward(): pl.pallas_call(head_backward_kernel, grid=(steps,), in_specs=[SMEM, down(...  39.4 us
    pallas_call x1, Pallas kernels, head_forward(): pl.pallas_call(functools.partial(head_forward_kernel, steps), grid=(steps...  24.5 us

profile of v4, /device:TPU:0, one launch (start us, length us, event | category | flops | bytes accessed | tf_op | source)
XLA Modules:
  0.0 225.3 jit_solution(8998286945708244049)
XLA Ops:
  0.6 1.8 pad_bitcast_fusion.own_ref
  2.5 48.5 %gather_weights.1 = (bf16[1696,512]{1,0:T(8,128)(2,1)}, f32[1,512]{1,0:T(1,128)}, f32[1,512]{1,0:T(1,128)}, bf16[1536,512]{1,0:T(8,128)(2,1)}, bf16[512,2048]{1,0:T(8,128)(2,1)}, /*index=5*/bf16[2048,512]{1,0:T(8,128)(2,1)}) custom-call(f32[920,128]{1,0:T(8,128)} %pad_bitcast_fusion.own_ref), custom_call_target="tpu_custom_call" | custom-call | tf_op jit(solution)/shard_map/gather_weights/pallas_call | solution.py:1006
  50.9 24.5 %head_forward.1 = (bf16[512,2048]{1,0:T(8,128)(2,1)}, f32[512,2048]{1,0:T(8,128)}, f32[8,2048]{1,0:T(8,128)}, f32[8,2048]{1,0:T(8,128)}, bf16[2048,128]{1,0:T(8,...) custom-call(s32[2,1024]{1,0:T(2,128)} %segment_smem.3, ...), custom_call_target="tpu_custom_call" | custom-call | flops 10000000000 | bytes 16000000 | tf_op jit(solution)/shard_map/head_forward/pallas_call | solution.py:475
  75.4 53.4 %middle.1 = (bf16[2048,512]{1,0:T(8,128)(2,1)}, f32[2048,512]{1,0:T(8,128)}, bf16[512,2048]{1,0:T(8,128)(2,1)}, f32[8,2048]{1,0:T(8,128)}, f32[24,2048]{1,0:T(8,...) custom-call(bf16[2048,512]{1,0:T(8,128)(2,1)} %x_ref.5, bf16[2048,512]{1,0:T(8,128)(2,1)} %dy_ref.1, ...), custom_call_target="tpu_custom_call" | custom-call | tf_op jit(solution)/shard_map/middle/pallas_call | solution.py:512
  128.9 39.4 %head_backward.1 = (f32[2048,512]{1,0:T(8,128)}, bf16[29328,128]{1,0:T(8,128)(2,1)}) custom-call(s32[2,1024]{1,0:T(2,128)} %segment_smem.3, bf16[2048,512]{1,0:T(8,128)(2,1)} %x_ref.5, f32[1,512]{1,0:T(1,128)} %get-tuple-element.42.gain_ref, bf16[1696,512]{1,0:T(8,128)(2,1)} %get-tuple-element.41.wall_ref, ...), custom_call_target="tpu_custom_call", output_to_operand_aliasing={{1}: (16, {})} | custom-call | flops 30000001024 | bytes 24000000 | tf_op jit(solution)/shard_map/head_backward/pallas_call | solution.py:563
  168.3 0.0 copy-start
  168.3 0.0 copy-start.1
  168.3 0.0 copy-start.2
  168.3 0.0 copy-start.3
  168.3 49.3 %reduce_grads.1 = (f32[916,128]{1,0:T(8,128)}, f32[1,128]{1,0:T(1,128)}, f32[2,512]{1,0:T(2,128)}) custom-call(bf16[29328,128]{1,0:T(8,128)(2,1)} %get-tuple-element.60.flat_ref, f32[1,128]{1,0:T(1,128)} %get-tuple-element.61.count_ref), custom_call_target="tpu_custom_call" | custom-call | tf_op jit(solution)/shard_map/reduce_grads/pallas_call | solution.py:1107
  217.7 1.2 slice.10
  219.6 1.1 multiply_bitcast_fusion
  220.7 0.0 copy-done
  220.7 0.0 copy-done.1
  220.7 0.0 copy-done.2
  220.7 0.0 copy-done.3
  220.7 0.0 copy-start.4
  220.8 2.6 %multiply_add_fusion = (f32[117152]{0:T(1024)}, f32[117152]{0:T(1024)}, f32[117152]{0:T(1024)}, f32[117152]{0:T(1024)}) fusion(f32[117152]{0:T(1024)S(1)} %copy-done.1, f32[117152]{0:T(1024)S(1)} %copy-done, f32[]{:T(128)} %bitcast.5, f32[117248]{0:T(1024)} %bitcast.8, f32[117152]{0:T(1024)S(1)} %copy-done.2, f32[117152]{0:T(1024)S(1)} %copy-done.3), kind=kLoop, calls=%fused_computation.3 | loop fusion | flops 1991584 | bytes 4217476 | tf_op jit(solution)/shard_map/add | solution.py:1171
  223.3 0.0 copy-done.4
  223.3 0.6 copy.20
Async XLA Ops:
  168.3 52.4 %copy-start = (f32[117152]{0:T(1024)S(1)}, f32[117152]{0:T(1024)}, u32[]{:S(2)}) copy-start(f32[117152]{0:T(1024)} %param.12) | copy-start | bytes 1405828
  168.3 52.4 %copy-start.1 = (f32[117152]{0:T(1024)S(1)}, f32[117152]{0:T(1024)}, u32[]{:S(2)}) copy-start(f32[117152]{0:T(1024)} %param.15) | copy-start | bytes 1405828
  168.3 52.4 %copy-start.2 = (f32[117152]{0:T(1024)S(1)}, f32[117152]{0:T(1024)}, u32[]{:S(2)}) copy-start(f32[117152]{0:T(1024)} %param.13) | copy-start | bytes 1405828
  168.3 52.4 %copy-start.3 = (f32[117152]{0:T(1024)S(1)}, f32[117152]{0:T(1024)}, u32[]{:S(2)}) copy-start(f32[117152]{0:T(1024)} %param.14) | copy-start | bytes 1405828
  220.7 2.6 %copy-start.4 = (f32[2,512]{1,0:T(2,128)S(1)}, f32[2,512]{1,0:T(2,128)}, u32[]{:S(2)}) copy-start(f32[2,512]{1,0:T(2,128)} %get-tuple-element.86) | copy-start | bytes 12292
